TPU v7x, 512 devices: a whole 4x8x8 slice. The times are simulated.
512 devices in a mesh: section: 8 (over y), fsdp: 8 (over z), dp: 8 (over x, core).
Axes of the slice: x: 4, y: 8, z: 8, core: 2. Of those that a mesh axis runs over, the one named last changes fastest.
Arguments:
- tokens_in: bfloat16 [4, 64, 128, 1664], P(None, ('fsdp', 'dp')), may hold values from -6 to 6
- keep_one: int32 [4, 64, 96], P(None, ('fsdp', 'dp')), may hold values from 0 to 127, as said below
- keep_two: int32 [4, 64, 64], P(None, ('fsdp', 'dp')), may hold values from 0 to 95, as said below
- keep_three: int32 [4, 64, 48], P(None, ('fsdp', 'dp')), may hold values from 0 to 63, as said below
- norm_gain: float32 [8, 1664], P('section'), may hold values from 0.5 to 1.5
- layer_scale: float32 [8, 1664], P('section'), may hold values from 0.3 to 1
- w_qkv: bfloat16 [8, 2496, 1664], P('section', ('fsdp', 'dp')), may hold values from -1 to 1
- w_out: bfloat16 [8, 832, 1664], P('section', ('fsdp', 'dp')), may hold values from -0.21875 to 0.21875
Outputs:
- stash: bfloat16 [8, 4, 64, 128, 1664], P('section', None, ('fsdp', 'dp'))
Inputs may be any that keep to these rules, and one draw needn't show every extreme that they name: `keep_one`: each list is strictly increasing. `keep_two`: each list is strictly increasing. `keep_three`: each list is strictly increasing.
All inputs are finite; a program needn't handle non-finite values.
Results may differ from a plain program's by a relative error of at most 0.015.
Values may be sent and summed in bfloat16 or wider, within the bound.
A program may use at most 128 MiB of HBM per device.

v0:
```python
import jax
import jax.numpy as jnp
from jax import lax
from jax.sharding import PartitionSpec as P

HDIM = 64


EPS = 1e-06


def shifted(value, axis, steps):
    count = lax.axis_size(axis)
    first, last = (max(0, -steps), min(count, count - steps))
    return lax.ppermute(value, axis, [(source, source + steps) for source in range(first, last)])


def norm_rows(tokens, gain):
    values = tokens.astype(jnp.float32)
    center = values - jnp.mean(values, axis=-1, keepdims=True)
    spread = jnp.mean(center * center, axis=-1, keepdims=True)
    return (center * lax.rsqrt(spread + EPS) * gain).astype(jnp.bfloat16)


def attend(tokens, gain, scale, proj_in, proj_out, live):
    rows = tokens.shape[0]
    width = proj_out.shape[0]
    heads = width // HDIM
    normed = norm_rows(tokens, gain)
    qkv = lax.dot_general(
        normed, proj_in, (((1,), (1,)), ((), ())), preferred_element_type=jnp.float32
    ).astype(jnp.bfloat16)
    query = qkv[:, :width].reshape(rows, heads, HDIM)
    keys = qkv[:, width : 2 * width].reshape(rows, heads, HDIM)
    values = qkv[:, 2 * width :].reshape(rows, heads, HDIM)
    scores = jnp.einsum("qhd,khd->hqk", query, keys, preferred_element_type=jnp.float32) * HDIM ** (
        -0.5
    )
    inside = jnp.arange(rows) < live
    scores = jnp.where(inside[None, None, :], scores, -1e30)
    top = jnp.max(scores, axis=-1, keepdims=True)
    expo = jnp.exp(scores - top)
    weights = (expo / jnp.sum(expo, axis=-1, keepdims=True)).astype(jnp.bfloat16)
    mixed = jnp.einsum("hqk,khd->qhd", weights, values, preferred_element_type=jnp.float32).astype(
        jnp.bfloat16
    )
    branch = jnp.dot(mixed.reshape(rows, width), proj_out, preferred_element_type=jnp.float32)
    result = tokens.astype(jnp.float32) + scale * branch
    return jnp.where(inside[:, None], result, 0.0).astype(jnp.bfloat16)


def prune(tokens, picks, level, depth_at):
    rows = tokens.shape[0]
    for depth in range(3):
        chosen = picks[depth]
        count = chosen.shape[0]
        full = jnp.concatenate([chosen, jnp.zeros((rows - count,), jnp.int32)])
        taken = jnp.take(tokens, full, axis=0)
        taken = jnp.where((jnp.arange(rows) < count)[:, None], taken, jnp.zeros_like(taken))
        tokens = jnp.where(level == depth_at[depth], taken, tokens)
    return tokens


def shards(tokens_in, keep_one, keep_two, keep_three, norm_gain, layer_scale, w_qkv, w_out):
    proj_in, proj_out = (
        lax.all_gather(w_qkv, ("fsdp", "dp"), axis=1, tiled=True),
        lax.all_gather(w_out, ("fsdp", "dp"), axis=1, tiled=True),
    )
    proj_in = proj_in[0]
    proj_out = proj_out[0]
    gain = norm_gain[0]
    scale = layer_scale[0]
    level = lax.axis_index("section")
    sections = lax.axis_size("section")
    micro = tokens_in.shape[0]
    rows = tokens_in.shape[2]
    features = tokens_in.shape[3]
    counts = [keep_one.shape[2], keep_two.shape[2], keep_three.shape[2]]
    depth_at = [(depth + 1) * sections // 4 for depth in range(3)]
    live_list = []
    for where_at in range(sections):
        current = rows
        for depth in range(3):
            if depth_at[depth] <= where_at:
                current = counts[depth]
        live_list.append(current)
    live_now = jnp.array(live_list, jnp.int32)[level]
    first_in = tokens_in[:, 0]
    lists = (keep_one[:, 0], keep_two[:, 0], keep_three[:, 0])

    def step(turn, carry):
        incoming, saved = carry
        index = turn - level
        active = jnp.logical_and(index >= 0, index < micro)
        slot = jnp.clip(index, 0, micro - 1)
        source = jnp.where(
            level == 0, lax.dynamic_index_in_dim(first_in, slot, 0, keepdims=False), incoming
        )
        picks = [lax.dynamic_index_in_dim(chosen, slot, 0, keepdims=False) for chosen in lists]

        def work(tokens):
            tokens = prune(tokens, picks, level, depth_at)
            return attend(tokens, gain, scale, proj_in, proj_out, live_now)

        def rest(tokens):
            return jnp.zeros_like(tokens)

        result = lax.cond(active, work, rest, source)
        before = lax.dynamic_index_in_dim(saved, slot, 0, keepdims=False)
        saved = lax.dynamic_update_index_in_dim(saved, jnp.where(active, result, before), slot, 0)
        incoming = shifted(result, "section", 1)
        return (incoming, saved)

    start = (
        jnp.zeros((rows, features), jnp.bfloat16),
        jnp.zeros((micro, rows, features), jnp.bfloat16),
    )
    final_in, saved = lax.fori_loop(0, sections + micro - 1, step, start)
    return saved[None, :, None]


def solution(mesh):
    return jax.shard_map(
        shards,
        mesh=mesh,
        in_specs=(
            P(None, ("fsdp", "dp"), None, None),
            P(None, ("fsdp", "dp"), None),
            P(None, ("fsdp", "dp"), None),
            P(None, ("fsdp", "dp"), None),
            P("section", None),
            P("section", None),
            P("section", ("fsdp", "dp"), None),
            P("section", ("fsdp", "dp"), None),
        ),
        out_specs=P("section", None, ("fsdp", "dp"), None, None),
        check_vma=False,
    )
```

profile of v0, /device:TPU:56, one launch (start us, length us, event | category | flops | bytes accessed | tf_op | source)
XLA Modules:
  0.0 575.1 jit_solution(8249085663550329180)
XLA Ops:
  6.5 1.5 copy.16
  8.1 1.8 copy.15
  11.2 89.9 %all-gather.5.cloned.1.call-done = bf16[1,832,1664]{2,0,1:T(2,128)(2,1)} async-done(((bf16[1,13,1664]{2,0,1:T(2,128)(2,1)}), bf16[1,832,1664]{2,0,1:T(2,128)(2,1)}) %all-gather.5.cloned.1.call-update) | async-done | bytes 2768912 | tf_op jit(solution)/shard_map/all_gather | solution.py:67
  101.1 4.6 copy.23
  105.7 100.9 %all-gather.3.cloned.1.call-done = bf16[1,2496,1664]{2,0,1:T(2,128)(2,1)} async-done(((bf16[1,39,1664]{2,0,1:T(2,128)(2,1)}), bf16[1,2496,1664]{2,0,1:T(2,128)(2,1)}) %all-gather.3.cloned.1.call-update) | async-done | bytes 8306704 | tf_op jit(solution)/shard_map/all_gather | solution.py:66
  206.7 11.6 %copy.22 = bf16[1,2496,1664]{2,1,0:T(8,128)(2,1)} copy(bf16[1,2496,1664]{2,0,1:T(2,128)(2,1)} %all-gather.3.cloned.1.call-done) | data formatting | bytes 16613376
  218.3 1.3 broadcast_in_dim.94
  220.4 347.8 %while.16 = (s32[]{:T(128)}, bf16[128,1664]{1,0:T(8,128)(2,1)}, bf16[4,128,1664]{2,1,0:T(8,128)(2,1)}, s32[]{:T(128)}, s32[]{:T(128)}, /*index=5*/pred[]{:T(512)...) while((s32[]{:T(128)}, bf16[128,1664]{1,0:T(8,128)(2,1)}, ...), condition=%wide.region_7.9_spmd, body=%wide.region_0.8_spmd.sunk | while | flops 1507565312 | bytes 40548756 | solution.py:118
  221.2 1.3 collective-permute-start
  224.4 11.0 %collective-permute-done = bf16[128,1664]{1,0:T(8,128)(2,1)} collective-permute-done((bf16[128,1664]{1,0:T(8,128)(2,1)}, bf16[128,1664]{1,0:T(8,128)(2,1)}, u32[]{:S(2)}, u32[]{:S(2)}) %collective-permute-start) | collective-permute-done | bytes 426016 | tf_op jit(solution)/shard_map/while/body/eval_jaxpr/ppermute | solution.py:15
  236.2 1.3 collective-permute-start
  239.4 10.2 %collective-permute-done = bf16[128,1664]{1,0:T(8,128)(2,1)} collective-permute-done((bf16[128,1664]{1,0:T(8,128)(2,1)}, bf16[128,1664]{1,0:T(8,128)(2,1)}, u32[]{:S(2)}, u32[]{:S(2)}) %collective-permute-start) | collective-permute-done | bytes 426016 | tf_op jit(solution)/shard_map/while/body/eval_jaxpr/ppermute | solution.py:15
  250.3 1.3 collective-permute-start
  253.5 9.2 %collective-permute-done = bf16[128,1664]{1,0:T(8,128)(2,1)} collective-permute-done((bf16[128,1664]{1,0:T(8,128)(2,1)}, bf16[128,1664]{1,0:T(8,128)(2,1)}, u32[]{:S(2)}, u32[]{:S(2)}) %collective-permute-start) | collective-permute-done | bytes 426016 | tf_op jit(solution)/shard_map/while/body/eval_jaxpr/ppermute | solution.py:15
  263.6 1.3 collective-permute-start
  266.8 9.5 %collective-permute-done = bf16[128,1664]{1,0:T(8,128)(2,1)} collective-permute-done((bf16[128,1664]{1,0:T(8,128)(2,1)}, bf16[128,1664]{1,0:T(8,128)(2,1)}, u32[]{:S(2)}, u32[]{:S(2)}) %collective-permute-start) | collective-permute-done | bytes 426016 | tf_op jit(solution)/shard_map/while/body/eval_jaxpr/ppermute | solution.py:15
  277.1 1.3 collective-permute-start
  280.3 8.5 %collective-permute-done = bf16[128,1664]{1,0:T(8,128)(2,1)} collective-permute-done((bf16[128,1664]{1,0:T(8,128)(2,1)}, bf16[128,1664]{1,0:T(8,128)(2,1)}, u32[]{:S(2)}, u32[]{:S(2)}) %collective-permute-start) | collective-permute-done | bytes 426016 | tf_op jit(solution)/shard_map/while/body/eval_jaxpr/ppermute | solution.py:15
  289.6 1.3 collective-permute-start
  292.8 7.7 %collective-permute-done = bf16[128,1664]{1,0:T(8,128)(2,1)} collective-permute-done((bf16[128,1664]{1,0:T(8,128)(2,1)}, bf16[128,1664]{1,0:T(8,128)(2,1)}, u32[]{:S(2)}, u32[]{:S(2)}) %collective-permute-start) | collective-permute-done | bytes 426016 | tf_op jit(solution)/shard_map/while/body/eval_jaxpr/ppermute | solution.py:15
  301.3 1.3 collective-permute-start
  304.5 138.8 %collective-permute-done = bf16[128,1664]{1,0:T(8,128)(2,1)} collective-permute-done((bf16[128,1664]{1,0:T(8,128)(2,1)}, bf16[128,1664]{1,0:T(8,128)(2,1)}, u32[]{:S(2)}, u32[]{:S(2)}) %collective-permute-start) | collective-permute-done | bytes 426016 | tf_op jit(solution)/shard_map/while/body/eval_jaxpr/ppermute | solution.py:15
  443.4 20.3 %conditional.2 = (bf16[128,1664]{1,0:T(8,128)(2,1)}) conditional(s32[]{:T(128)} %convert_element_type.64, () %tuple.54, (s32[]{:T(128)}, s32[]{:T(128)}, pred[]{:T(512)}, bf16[4,128,1664]{2,1,0:T(8,128)(2,1)}, s32[]{:T(128)}, /*index=5*/bf16[128,1664]{1,0:T(8,128)(2,1)}, s32[4,96]{1,0:T(4,128)}, s32[4,64]{1,0:T(4,128)}, s32[4,48]{1,0:T(4,128)}, ...), branch_computations={%region_1.1_spmd, %region_2.7_spmd} | conditional | flops 1507352320 | bytes 36714016 | solution.py:108
  450.5 5.8 %convolution_convert_fusion = bf16[128,2496]{0,1:T(8,128)(2,1)S(1)} fusion(bf16[2496,1664]{1,0:T(8,128)(2,1)} %get-tuple-element.383, bf16[128,1664]{1,0:T(8,128)(2,1)S(1)} %get-tuple-element.431, f32[1664]{0:T(1024)S(1)} %reduce.1, f32[128]{0:T(128)S(1)} %add_rsqrt_fusion, f32[128]{0:T(128)S(1)} %broadcast_multiply_fusion), kind=kOutput, calls=%fused_computation.4 | convolution fusion | flops 1064640512 | bytes 9379328 | tf_op jit(solution)/shard_map/while/body/eval_jaxpr/cond/branch_1_fun/dot_general | solution.py:30
  458.6 2.6 convolution_convert_fusion.1
  461.3 2.4 fusion.3
  463.7 1.3 collective-permute-start
  466.0 1.9 bitcast_dynamic-update-slice_fusion.2
  467.9 6.5 %collective-permute-done = bf16[128,1664]{1,0:T(8,128)(2,1)} collective-permute-done((bf16[128,1664]{1,0:T(8,128)(2,1)}, bf16[128,1664]{1,0:T(8,128)(2,1)}, u32[]{:S(2)}, u32[]{:S(2)}) %collective-permute-start) | collective-permute-done | bytes 426016 | tf_op jit(solution)/shard_map/while/body/eval_jaxpr/ppermute | solution.py:15
  474.4 20.3 %conditional.2 = (bf16[128,1664]{1,0:T(8,128)(2,1)}) conditional(s32[]{:T(128)} %convert_element_type.64, () %tuple.54, (s32[]{:T(128)}, s32[]{:T(128)}, pred[]{:T(512)}, bf16[4,128,1664]{2,1,0:T(8,128)(2,1)}, s32[]{:T(128)}, /*index=5*/bf16[128,1664]{1,0:T(8,128)(2,1)}, s32[4,96]{1,0:T(4,128)}, s32[4,64]{1,0:T(4,128)}, s32[4,48]{1,0:T(4,128)}, ...), branch_computations={%region_1.1_spmd, %region_2.7_spmd} | conditional | flops 1507352320 | bytes 36714016 | solution.py:108
  481.6 5.8 %convolution_convert_fusion = bf16[128,2496]{0,1:T(8,128)(2,1)S(1)} fusion(bf16[2496,1664]{1,0:T(8,128)(2,1)} %get-tuple-element.383, bf16[128,1664]{1,0:T(8,128)(2,1)S(1)} %get-tuple-element.431, f32[1664]{0:T(1024)S(1)} %reduce.1, f32[128]{0:T(128)S(1)} %add_rsqrt_fusion, f32[128]{0:T(128)S(1)} %broadcast_multiply_fusion), kind=kOutput, calls=%fused_computation.4 | convolution fusion | flops 1064640512 | bytes 9379328 | tf_op jit(solution)/shard_map/while/body/eval_jaxpr/cond/branch_1_fun/dot_general | solution.py:30
  489.7 2.6 convolution_convert_fusion.1
  492.3 2.4 fusion.3
  494.7 1.3 collective-permute-start
  497.0 1.9 bitcast_dynamic-update-slice_fusion.2
  498.9 6.8 %collective-permute-done = bf16[128,1664]{1,0:T(8,128)(2,1)} collective-permute-done((bf16[128,1664]{1,0:T(8,128)(2,1)}, bf16[128,1664]{1,0:T(8,128)(2,1)}, u32[]{:S(2)}, u32[]{:S(2)}) %collective-permute-start) | collective-permute-done | bytes 426016 | tf_op jit(solution)/shard_map/while/body/eval_jaxpr/ppermute | solution.py:15
  505.7 20.3 %conditional.2 = (bf16[128,1664]{1,0:T(8,128)(2,1)}) conditional(s32[]{:T(128)} %convert_element_type.64, () %tuple.54, (s32[]{:T(128)}, s32[]{:T(128)}, pred[]{:T(512)}, bf16[4,128,1664]{2,1,0:T(8,128)(2,1)}, s32[]{:T(128)}, /*index=5*/bf16[128,1664]{1,0:T(8,128)(2,1)}, s32[4,96]{1,0:T(4,128)}, s32[4,64]{1,0:T(4,128)}, s32[4,48]{1,0:T(4,128)}, ...), branch_computations={%region_1.1_spmd, %region_2.7_spmd} | conditional | flops 1507352320 | bytes 36714016 | solution.py:108
  512.9 5.8 %convolution_convert_fusion = bf16[128,2496]{0,1:T(8,128)(2,1)S(1)} fusion(bf16[2496,1664]{1,0:T(8,128)(2,1)} %get-tuple-element.383, bf16[128,1664]{1,0:T(8,128)(2,1)S(1)} %get-tuple-element.431, f32[1664]{0:T(1024)S(1)} %reduce.1, f32[128]{0:T(128)S(1)} %add_rsqrt_fusion, f32[128]{0:T(128)S(1)} %broadcast_multiply_fusion), kind=kOutput, calls=%fused_computation.4 | convolution fusion | flops 1064640512 | bytes 9379328 | tf_op jit(solution)/shard_map/while/body/eval_jaxpr/cond/branch_1_fun/dot_general | solution.py:30
  521.0 2.6 convolution_convert_fusion.1
  523.7 2.4 fusion.3
  528.4 1.9 bitcast_dynamic-update-slice_fusion.2
  530.3 7.3 %collective-permute-done = bf16[128,1664]{1,0:T(8,128)(2,1)} collective-permute-done((bf16[128,1664]{1,0:T(8,128)(2,1)}, bf16[128,1664]{1,0:T(8,128)(2,1)}, u32[]{:S(2)}, u32[]{:S(2)}) %collective-permute-start) | collective-permute-done | bytes 426016 | tf_op jit(solution)/shard_map/while/body/eval_jaxpr/ppermute | solution.py:15
  537.6 20.3 %conditional.2 = (bf16[128,1664]{1,0:T(8,128)(2,1)}) conditional(s32[]{:T(128)} %convert_element_type.64, () %tuple.54, (s32[]{:T(128)}, s32[]{:T(128)}, pred[]{:T(512)}, bf16[4,128,1664]{2,1,0:T(8,128)(2,1)}, s32[]{:T(128)}, /*index=5*/bf16[128,1664]{1,0:T(8,128)(2,1)}, s32[4,96]{1,0:T(4,128)}, s32[4,64]{1,0:T(4,128)}, s32[4,48]{1,0:T(4,128)}, ...), branch_computations={%region_1.1_spmd, %region_2.7_spmd} | conditional | flops 1507352320 | bytes 36714016 | solution.py:108
  544.8 5.8 %convolution_convert_fusion = bf16[128,2496]{0,1:T(8,128)(2,1)S(1)} fusion(bf16[2496,1664]{1,0:T(8,128)(2,1)} %get-tuple-element.383, bf16[128,1664]{1,0:T(8,128)(2,1)S(1)} %get-tuple-element.431, f32[1664]{0:T(1024)S(1)} %reduce.1, f32[128]{0:T(128)S(1)} %add_rsqrt_fusion, f32[128]{0:T(128)S(1)} %broadcast_multiply_fusion), kind=kOutput, calls=%fused_computation.4 | convolution fusion | flops 1064640512 | bytes 9379328 | tf_op jit(solution)/shard_map/while/body/eval_jaxpr/cond/branch_1_fun/dot_general | solution.py:30
  552.9 2.6 convolution_convert_fusion.1
  555.5 2.4 fusion.3
  560.2 1.9 bitcast_dynamic-update-slice_fusion.2
  562.1 6.1 %collective-permute-done = bf16[128,1664]{1,0:T(8,128)(2,1)} collective-permute-done((bf16[128,1664]{1,0:T(8,128)(2,1)}, bf16[128,1664]{1,0:T(8,128)(2,1)}, u32[]{:S(2)}, u32[]{:S(2)}) %collective-permute-start) | collective-permute-done | bytes 426016 | tf_op jit(solution)/shard_map/while/body/eval_jaxpr/ppermute | solution.py:15
  (156 shorter events, 70.9 us)
Async XLA Ops:
  6.5 94.6 %all-gather.5.cloned.1.call-start = ((), (), s32[]{:S(2)}) async-start(), calls=%async_computation.1 | async-start | bytes 5624320 | tf_op jit(solution)/shard_map/all_gather | solution.py:67
  8.1 198.6 %all-gather.3.cloned.1.call-start = ((), (), s32[]{:S(2)}) async-start(), calls=%async_computation | async-start | bytes 16872960 | tf_op jit(solution)/shard_map/all_gather | solution.py:66
  218.3 2.1 copy-start.1
  218.3 2.1 copy-start.2
  221.2 14.2 %collective-permute-start = (bf16[128,1664]{1,0:T(8,128)(2,1)}, bf16[128,1664]{1,0:T(8,128)(2,1)}, u32[]{:S(2)}, u32[]{:S(2)}) collective-permute-start(bf16[128,1664]{1,0:T(8,128)(2,1)} %get-tuple-element.583), channel_id=1, source_target_pairs={{0,64},{64,128},{128,192},{192,256},{256,320},{320,384},{384,448},... | collective-permute-start | bytes 1277960 | tf_op jit(solution)/shard_map/while/body/eval_jaxpr/ppermute | solution.py:15
  236.2 13.4 %collective-permute-start = (bf16[128,1664]{1,0:T(8,128)(2,1)}, bf16[128,1664]{1,0:T(8,128)(2,1)}, u32[]{:S(2)}, u32[]{:S(2)}) collective-permute-start(bf16[128,1664]{1,0:T(8,128)(2,1)} %get-tuple-element.583), channel_id=1, source_target_pairs={{0,64},{64,128},{128,192},{192,256},{256,320},{320,384},{384,448},... | collective-permute-start | bytes 1277960 | tf_op jit(solution)/shard_map/while/body/eval_jaxpr/ppermute | solution.py:15
  250.3 12.4 %collective-permute-start = (bf16[128,1664]{1,0:T(8,128)(2,1)}, bf16[128,1664]{1,0:T(8,128)(2,1)}, u32[]{:S(2)}, u32[]{:S(2)}) collective-permute-start(bf16[128,1664]{1,0:T(8,128)(2,1)} %get-tuple-element.583), channel_id=1, source_target_pairs={{0,64},{64,128},{128,192},{192,256},{256,320},{320,384},{384,448},... | collective-permute-start | bytes 1277960 | tf_op jit(solution)/shard_map/while/body/eval_jaxpr/ppermute | solution.py:15
  263.6 12.8 %collective-permute-start = (bf16[128,1664]{1,0:T(8,128)(2,1)}, bf16[128,1664]{1,0:T(8,128)(2,1)}, u32[]{:S(2)}, u32[]{:S(2)}) collective-permute-start(bf16[128,1664]{1,0:T(8,128)(2,1)} %get-tuple-element.583), channel_id=1, source_target_pairs={{0,64},{64,128},{128,192},{192,256},{256,320},{320,384},{384,448},... | collective-permute-start | bytes 1277960 | tf_op jit(solution)/shard_map/while/body/eval_jaxpr/ppermute | solution.py:15
  277.1 11.7 %collective-permute-start = (bf16[128,1664]{1,0:T(8,128)(2,1)}, bf16[128,1664]{1,0:T(8,128)(2,1)}, u32[]{:S(2)}, u32[]{:S(2)}) collective-permute-start(bf16[128,1664]{1,0:T(8,128)(2,1)} %get-tuple-element.583), channel_id=1, source_target_pairs={{0,64},{64,128},{128,192},{192,256},{256,320},{320,384},{384,448},... | collective-permute-start | bytes 1277960 | tf_op jit(solution)/shard_map/while/body/eval_jaxpr/ppermute | solution.py:15
  289.6 10.9 %collective-permute-start = (bf16[128,1664]{1,0:T(8,128)(2,1)}, bf16[128,1664]{1,0:T(8,128)(2,1)}, u32[]{:S(2)}, u32[]{:S(2)}) collective-permute-start(bf16[128,1664]{1,0:T(8,128)(2,1)} %get-tuple-element.583), channel_id=1, source_target_pairs={{0,64},{64,128},{128,192},{192,256},{256,320},{320,384},{384,448},... | collective-permute-start | bytes 1277960 | tf_op jit(solution)/shard_map/while/body/eval_jaxpr/ppermute | solution.py:15
  301.3 142.0 %collective-permute-start = (bf16[128,1664]{1,0:T(8,128)(2,1)}, bf16[128,1664]{1,0:T(8,128)(2,1)}, u32[]{:S(2)}, u32[]{:S(2)}) collective-permute-start(bf16[128,1664]{1,0:T(8,128)(2,1)} %get-tuple-element.583), channel_id=1, source_target_pairs={{0,64},{64,128},{128,192},{192,256},{256,320},{320,384},{384,448},... | collective-permute-start | bytes 1277960 | tf_op jit(solution)/shard_map/while/body/eval_jaxpr/ppermute | solution.py:15
  458.6 2.7 copy-start
  463.7 10.7 %collective-permute-start = (bf16[128,1664]{1,0:T(8,128)(2,1)}, bf16[128,1664]{1,0:T(8,128)(2,1)}, u32[]{:S(2)}, u32[]{:S(2)}) collective-permute-start(bf16[128,1664]{1,0:T(8,128)(2,1)} %get-tuple-element.583), channel_id=1, source_target_pairs={{0,64},{64,128},{128,192},{192,256},{256,320},{320,384},{384,448},... | collective-permute-start | bytes 1277960 | tf_op jit(solution)/shard_map/while/body/eval_jaxpr/ppermute | solution.py:15
  489.7 2.7 copy-start
  494.7 11.0 %collective-permute-start = (bf16[128,1664]{1,0:T(8,128)(2,1)}, bf16[128,1664]{1,0:T(8,128)(2,1)}, u32[]{:S(2)}, u32[]{:S(2)}) collective-permute-start(bf16[128,1664]{1,0:T(8,128)(2,1)} %get-tuple-element.583), channel_id=1, source_target_pairs={{0,64},{64,128},{128,192},{192,256},{256,320},{320,384},{384,448},... | collective-permute-start | bytes 1277960 | tf_op jit(solution)/shard_map/while/body/eval_jaxpr/ppermute | solution.py:15
  521.0 2.7 copy-start
  526.0 11.5 %collective-permute-start = (bf16[128,1664]{1,0:T(8,128)(2,1)}, bf16[128,1664]{1,0:T(8,128)(2,1)}, u32[]{:S(2)}, u32[]{:S(2)}) collective-permute-start(bf16[128,1664]{1,0:T(8,128)(2,1)} %get-tuple-element.583), channel_id=1, source_target_pairs={{0,64},{64,128},{128,192},{192,256},{256,320},{320,384},{384,448},... | collective-permute-start | bytes 1277960 | tf_op jit(solution)/shard_map/while/body/eval_jaxpr/ppermute | solution.py:15
  552.9 2.7 copy-start
  557.9 10.3 %collective-permute-start = (bf16[128,1664]{1,0:T(8,128)(2,1)}, bf16[128,1664]{1,0:T(8,128)(2,1)}, u32[]{:S(2)}, u32[]{:S(2)}) collective-permute-start(bf16[128,1664]{1,0:T(8,128)(2,1)} %get-tuple-element.583), channel_id=1, source_target_pairs={{0,64},{64,128},{128,192},{192,256},{256,320},{320,384},{384,448},... | collective-permute-start | bytes 1277960 | tf_op jit(solution)/shard_map/while/body/eval_jaxpr/ppermute | solution.py:15
Sparse Core Ops, SparseCore 0:
  10.6 90.4 all-gather.4
  104.4 102.2 all-gather.2
where the time goes:
time: 577 us; the launch traced here: 575 us
  waiting for transfers between devices  413 us (72%)
  local copies, waits for them, and re-layouts  59.6 us (10%)
  matrix products  49.8 us (9%)
  other arithmetic  24.8 us (4%)
  starting transfers between devices  14.1 us (2%)
  between operations  13.4 us (2%)
    ppermute x11, waiting for transfers between devices, shifted(): lax.ppermute(value, axis, [(source, source + steps) for source in range(f...  222 us
    all_gather x1, waiting for transfers between devices, shards(): lax.all_gather(w_qkv, ('fsdp', 'dp'), axis=1, tiled=True)  101 us
    all_gather x1, waiting for transfers between devices, shards(): lax.all_gather(w_out, ('fsdp', 'dp'), axis=1, tiled=True)  89.9 us
    dot_general x4, matrix products, attend(): lax.dot_general(normed, proj_in, (((1,), (1,)), ((), ())), preferred_elem...  23.1 us
    unnamed x8, local copies, waits for them, and re-layouts  19.6 us
    ppermute x11, starting transfers between devices, shifted(): lax.ppermute(value, axis, [(source, source + steps) for source in range(f...  14.1 us
    dynamic_update_slice x11, other arithmetic, step(): lax.dynamic_update_index_in_dim(saved, jnp.where(active, result, before),...  13.6 us
  transfers between devices with their start and end apart: 13, of which 13 were waited for; matrix products, arithmetic and copies ran while one was open for 6% of the time, Pallas kernels for 0%

commit v1 on v0

v1 whole, which is shorter than its diff:
```python
import functools

import jax
import jax.numpy as jnp
import numpy as np
from jax import lax
from jax.experimental import pallas as pl
from jax.experimental.pallas import tpu as pltpu
from jax.sharding import PartitionSpec as P

MESH = pl.DeviceIdType.MESH
HDIM = 64
EPS = 1e-06
LANE = 128
MAIN = 48
REST = 64
A_ROWS = 272
A_HALF = 144
B_HALF = 208


def compaction(rows_in, rows_out, tiles):
    pad_in = -(-8 * rows_in // 16) * 16
    pad_out = -(-8 * rows_out // 16) * 16
    first = MAIN - rows_in
    left = rows_out - first
    every = np.zeros((pad_in + pad_out, 8 * MAIN + 8 * left), np.float32)
    rest = np.zeros((tiles * 8 * left, 8 * REST), np.float32)
    for core in range(2):
        for x in range(4):
            place, rank = core * 4 + x, x * 2 + core
            for i in range(rows_in):
                every[rank * rows_in + i, place * MAIN + i] = 1
            for i in range(first):
                every[pad_in + rank * rows_out + i, place * MAIN + rows_in + i] = 1
            for i in range(left):
                every[pad_in + rank * rows_out + first + i, 8 * MAIN + place * left + i] = 1
                for tile in range(tiles):
                    rest[tile * 8 * left + place * left + i, place * REST + tile * left + i] = 1
    return every, rest


def kernel(
    tok_ref,
    one_ref,
    two_ref,
    three_ref,
    gain_ref,
    scale_ref,
    wq_ref,
    wo_ref,
    every_ref,
    rest_ref,
    out_ref,
    gbuf,
    wd,
    wod,
    recv,
    res,
    pruned,
    picks,
    stage,
    small,
    normed,
    qkv,
    mixed,
    tok_sem,
    out_sem,
    z_send,
    z_recv,
    xa_send,
    xa_recv,
    xb_send,
    xb_recv,
    sib_send,
    sib_recv,
    t_send,
    t_recv,
):
    micro, rows, feats = tok_ref.shape
    tiles = feats // LANE
    rows_in, rows_out = wq_ref.shape[0], wo_ref.shape[0]
    group_in, group_out = 8 * rows_in, 8 * rows_out
    width = 64 * rows_out
    heads = width // HDIM
    left = rows_in + rows_out - MAIN
    level = lax.axis_index("section")
    z = lax.axis_index("fsdp")
    dp = lax.axis_index("dp")
    x = dp // 2
    core = dp - 2 * x

    def zat(step):
        return lax.rem(z + step + 8, 8)

    def xat(step):
        return lax.rem(x + step + 4, 4)

    x_plus, x_minus = (level, z, xat(1) * 2 + core), (level, z, xat(-1) * 2 + core)
    z_plus, z_minus = (level, zat(1), dp), (level, zat(-1), dp)
    sibling = (level, z, x * 2 + 1 - core)
    y_plus, y_minus = (lax.rem(level + 1, 8), z, dp), (lax.rem(level + 7, 8), z, dp)

    recv[...] = jnp.zeros_like(recv)
    barrier = pltpu.get_barrier_semaphore()
    partners = (x_plus, x_minus, z_plus, z_minus, sibling, y_plus, y_minus)
    for partner in partners:
        pl.semaphore_signal(barrier, inc=1, device_id=partner, device_id_type=MESH)

    stage[pl.ds(0, rows_in), :] = wq_ref[...].astype(jnp.float32)
    stage[pl.ds(rows_in, rows_out), :] = wo_ref[...].astype(jnp.float32)
    small[...] = jnp.zeros_like(small)
    for tile in range(tiles):
        lanes = slice(tile * LANE, (tile + 1) * LANE)
        gbuf[core, z, x, tile * MAIN : (tile + 1) * MAIN, :] = stage[0:MAIN, lanes].astype(jnp.bfloat16)
        small[tile * left : (tile + 1) * left, :] = stage[MAIN : MAIN + left, lanes]
    gbuf[core, z, x, tiles * MAIN : tiles * MAIN + REST, :] = small[...].astype(jnp.bfloat16)

    pl.semaphore_wait(barrier, len(partners))

    total = tiles * MAIN + REST
    A, A1, A2 = pl.ds(0, A_ROWS), pl.ds(0, A_HALF), pl.ds(A_HALF, A_ROWS - A_HALF)
    B, B1, B2 = (
        pl.ds(A_ROWS, total - A_ROWS),
        pl.ds(A_ROWS, B_HALF),
        pl.ds(A_ROWS + B_HALF, total - A_ROWS - B_HALF),
    )

    started = []

    def send(part, ss, rs, to):
        copy = pltpu.make_async_remote_copy(
            src_ref=part, dst_ref=part, send_sem=ss, recv_sem=rs, device_id=to, device_id_type=MESH
        )
        copy.start()
        started.append(copy)

    def arrive(part, ss, rs):
        pltpu.make_async_remote_copy(
            src_ref=part, dst_ref=part, send_sem=ss, recv_sem=rs, device_id=z_plus, device_id_type=MESH
        ).wait_recv()

    zdir = (z_plus, z_minus)
    xdir = (x_plus, x_minus)
    sign = (-1, 1)

    def at(dz, dx, part):
        return gbuf.at[core, zat(dz), xat(dx), part]

    def row(dz, part):
        return gbuf.at[core, zat(dz), :, part]

    def z_go(kind, d, k, part):
        send(part, z_send.at[kind, d, k - 1], z_recv.at[kind, d, k - 1], zdir[d])

    def z_come(kind, d, k, part):
        arrive(part, z_send.at[kind, d, k - 1], z_recv.at[kind, d, k - 1])

    def xa_go(d, k, part):
        send(part, xa_send.at[d, k - 1], xa_recv.at[d, k - 1], xdir[d])

    def xa_come(d, k, part):
        arrive(part, xa_send.at[d, k - 1], xa_recv.at[d, k - 1])

    def xb_go(dz, d, k, part):
        i = dz % 8
        send(part, xb_send.at[i, d, k - 1], xb_recv.at[i, d, k - 1], xdir[d])

    def xb_come(dz, d, k, part):
        i = dz % 8
        arrive(part, xb_send.at[i, d, k - 1], xb_recv.at[i, d, k - 1])

    def x_spread(dz):
        for d in range(2):
            xb_go(dz, d, 1, at(dz, 0, B))

    def x_relay(dz):
        for d in range(2):
            xb_come(dz, d, 1, at(dz, sign[d], B))
            xb_go(dz, d, 2, at(dz, sign[d], (B1, B2)[d]))

    def x_end(dz):
        for d in range(2):
            xb_come(dz, d, 2, at(dz, 2 * sign[d], (B1, B2)[d]))

    def to_sibling(dz):
        i = dz % 8
        send(gbuf.at[core, zat(dz)], sib_send.at[i], sib_recv.at[i], sibling)

    def pack(dz):
        i = dz % 8
        g = zat(dz)
        arrive(gbuf.at[1 - core, g], sib_send.at[i], sib_recv.at[i])
        tail = gbuf[:, g, :, tiles * MAIN : tiles * MAIN + REST, :].reshape(8 * REST, LANE)
        tail = jnp.dot(rest_ref[...], tail, preferred_element_type=jnp.float32).astype(jnp.bfloat16)
        for tile in range(0, tiles, 2):
            count = min(2, tiles - tile)
            columns = [
                jnp.concatenate(
                    [
                        gbuf[:, g, :, t * MAIN : (t + 1) * MAIN, :].reshape(8 * MAIN, LANE),
                        tail[t * 8 * left : (t + 1) * 8 * left, :],
                    ],
                    axis=0,
                )
                for t in range(tile, tile + count)
            ]
            block = columns[0] if count == 1 else jnp.concatenate(columns, axis=1)
            dense = jnp.dot(every_ref[...], block, preferred_element_type=jnp.float32).astype(jnp.bfloat16)
            lanes = slice(tile * LANE, (tile + count) * LANE)
            pad_in = wd.shape[1]
            wd[g, :, lanes] = dense[:pad_in]
            wod[g, :, lanes] = dense[pad_in:]

    for d in range(2):
        z_go(1, d, 1, at(0, 0, B))
    for d in range(2):
        xa_go(d, 1, at(0, 0, A))
    x_spread(0)

    @pl.when(level == 0)
    def _():
        pltpu.make_async_copy(tok_ref, recv, tok_sem).start()

    picks[...] = jnp.zeros_like(picks)
    for here, chosen in ((1, one_ref), (3, two_ref), (5, three_ref)):

        @pl.when(level == here)
        def _():
            count = chosen.shape[1]
            place = lax.broadcasted_iota(jnp.int32, (rows, count), 0)
            for m in range(micro):
                hit = place == chosen[m : m + 1, :]
                picks[m, :, 0:count] = jnp.where(hit, 1.0, 0.0).astype(jnp.bfloat16)

    for d in range(2):
        xa_come(d, 1, at(0, sign[d], A))
        xa_go(d, 2, at(0, sign[d], (A1, A2)[d]))

    def z_relay(k):
        for d in range(2):
            if k < 4:
                z_come(1, d, k, at(sign[d] * k, 0, B))
                z_go(1, d, k + 1, at(sign[d] * k, 0, B if k < 3 else (B1, B2)[d]))
                x_spread(sign[d] * k)
            else:
                z_come(1, d, k, at(4, 0, (B1, B2)[d]))
        if k == 4:
            x_spread(4)

    def za_relay(k):
        for d in range(2):
            if k < 4:
                z_come(0, d, k, row(sign[d] * k, A))
                z_go(0, d, k + 1, row(sign[d] * k, A if k < 3 else (A1, A2)[d]))
            else:
                z_come(0, d, k, row(4, (A1, A2)[d]))

    z_relay(1)
    x_relay(0)
    for d in range(2):
        xa_come(d, 2, at(0, 2, (A1, A2)[d]))
    for d in range(2):
        z_go(0, d, 1, row(0, A))
    z_relay(2)
    x_relay(-1)
    x_relay(1)
    z_relay(3)
    za_relay(1)
    x_relay(-2)
    x_relay(2)
    z_relay(4)
    x_end(0)
    to_sibling(0)
    za_relay(2)
    x_relay(-3)
    x_relay(3)
    x_end(-1)
    x_end(1)
    to_sibling(-1)
    to_sibling(1)
    pack(0)
    za_relay(3)
    x_relay(4)
    x_end(-2)
    x_end(2)
    to_sibling(-2)
    to_sibling(2)
    pack(-1)
    pack(1)
    x_end(-3)
    x_end(3)
    to_sibling(-3)
    to_sibling(3)
    pack(-2)
    pack(2)
    za_relay(4)
    x_end(4)
    to_sibling(4)
    pack(-3)
    pack(3)
    pack(4)

    live = rows - 32 * (level >= 2).astype(jnp.int32)
    live = live - 32 * (level >= 4).astype(jnp.int32) - 16 * (level >= 6).astype(jnp.int32)

    def token_copy(m, source, count):
        return pltpu.make_async_remote_copy(
            src_ref=source.at[m, pl.ds(0, count)],
            dst_ref=recv.at[m, pl.ds(0, count)],
            send_sem=t_send.at[m],
            recv_sem=t_recv.at[m],
            device_id=y_plus,
            device_id_type=MESH,
        )

    @pl.when(level == 0)
    def _():
        pltpu.make_async_copy(tok_ref, recv, tok_sem).wait()

    counts = (one_ref.shape[1], two_ref.shape[1], three_ref.shape[1])
    incoming = ((1, 1, rows), (2, 3, counts[0]), (4, 5, counts[1]), (6, 7, counts[2]))

    def body(m, carry):
        for low, high, count in incoming:

            @pl.when(jnp.logical_and(level >= low, level <= high))
            def _():
                token_copy(m, recv, count).wait_recv()

        values = recv[m].astype(jnp.float32)
        center = values - jnp.mean(values, axis=-1, keepdims=True)
        spread = jnp.mean(center * center, axis=-1, keepdims=True)
        normed[...] = (center * lax.rsqrt(spread + EPS) * gain_ref[...]).astype(jnp.bfloat16)

        def project(g, carry):
            part = lax.dot_general(
                wd[g], normed[...], (((1,), (1,)), ((), ())), preferred_element_type=jnp.float32
            )
            start = pl.multiple_of(g * group_in, 8)
            qkv[pl.ds(start, group_in), :] = part[:group_in]
            return carry

        lax.fori_loop(0, 8, project, 0)

        inside = lax.broadcasted_iota(jnp.int32, (rows, rows), 0) < live
        for h in range(heads):
            low = h * HDIM
            query = (qkv[low : low + HDIM, :].astype(jnp.bfloat16) * jnp.bfloat16(HDIM**-0.5))
            keys = qkv[width + low : width + low + HDIM, :].astype(jnp.bfloat16)
            vals = qkv[2 * width + low : 2 * width + low + HDIM, :].astype(jnp.bfloat16)
            scores = lax.dot_general(
                keys, query, (((0,), (0,)), ((), ())), preferred_element_type=jnp.float32
            )
            scores = jnp.where(inside, scores, -1e30)
            top = jnp.max(scores, axis=0, keepdims=True)
            expo = jnp.exp(scores - top)
            weights = (expo / jnp.sum(expo, axis=0, keepdims=True)).astype(jnp.bfloat16)
            mixed[low : low + HDIM, :] = jnp.dot(vals, weights, preferred_element_type=jnp.float32)

        parts = []
        gap = jnp.zeros((wod.shape[1] - group_out, rows), jnp.float32)
        for g in range(8):
            parts.append(mixed[g * group_out : (g + 1) * group_out, :])
            if gap.shape[0]:
                parts.append(gap)
        across = jnp.transpose(jnp.concatenate(parts, axis=0)).astype(jnp.bfloat16)
        alive = lax.broadcasted_iota(jnp.int32, (rows, LANE), 0) < live
        for low in range(0, feats, 4 * LANE):
            size = min(4 * LANE, feats - low)
            lanes = slice(low, low + size)
            block = wod[:, :, lanes].reshape(8 * wod.shape[1], size)
            branch = jnp.dot(across, block, preferred_element_type=jnp.float32)
            sums = recv[m, :, lanes].astype(jnp.float32) + scale_ref[:, lanes] * branch
            sums = jnp.where(alive[:, :1], sums, 0.0)
            res[m, :, lanes] = sums.astype(jnp.bfloat16)

        pltpu.make_async_copy(res.at[m], out_ref.at[m], out_sem.at[m]).start()

        for here, count in ((0, rows), (2, counts[0]), (4, counts[1]), (6, counts[2])):

            @pl.when(level == here)
            def _():
                token_copy(m, res, count).start()

        for here, count in ((1, counts[0]), (3, counts[1]), (5, counts[2])):

            @pl.when(level == here)
            def _():
                for low in range(0, feats, 4 * LANE):
                    size = min(4 * LANE, feats - low)
                    lanes = slice(low, low + size)
                    taken = lax.dot_general(
                        picks[m],
                        res[m, :, lanes],
                        (((0,), (0,)), ((), ())),
                        preferred_element_type=jnp.float32,
                    )
                    pruned[m, :, lanes] = taken.astype(jnp.bfloat16)
                token_copy(m, pruned, count).start()

        return carry

    lax.fori_loop(0, micro, body, 0)

    for copy in started:
        copy.wait_send()

    def finish(m, carry):
        pltpu.make_async_copy(res.at[m], out_ref.at[m], out_sem.at[m]).wait()
        for here, count in ((0, rows), (2, counts[0]), (4, counts[1]), (6, counts[2])):

            @pl.when(level == here)
            def _():
                token_copy(m, res, count).wait_send()

        for here, count in ((1, counts[0]), (3, counts[1]), (5, counts[2])):

            @pl.when(level == here)
            def _():
                token_copy(m, pruned, count).wait_send()

        return carry

    lax.fori_loop(0, micro, finish, 0)


def shards(tokens_in, keep_one, keep_two, keep_three, norm_gain, layer_scale, w_qkv, w_out):
    micro, _, rows, feats = tokens_in.shape
    rows_in, rows_out = w_qkv.shape[1], w_out.shape[1]
    tiles = feats // LANE
    every, rest = compaction(rows_in, rows_out, tiles)
    pad_in = -(-8 * rows_in // 16) * 16
    pad_out = -(-8 * rows_out // 16) * 16
    vmem = pl.BlockSpec(memory_space=pltpu.VMEM)
    dma = pltpu.SemaphoreType.DMA
    stash = pl.pallas_call(
        kernel,
        out_shape=jax.ShapeDtypeStruct((micro, rows, feats), jnp.bfloat16),
        in_specs=[pl.BlockSpec(memory_space=pl.ANY)] + [vmem] * 9,
        out_specs=pl.BlockSpec(memory_space=pl.ANY),
        scratch_shapes=[
            pltpu.VMEM((2, 8, 4, tiles * MAIN + REST, LANE), jnp.bfloat16),
            pltpu.VMEM((8, pad_in, feats), jnp.bfloat16),
            pltpu.VMEM((8, pad_out, feats), jnp.bfloat16),
            pltpu.VMEM((micro, rows, feats), jnp.bfloat16),
            pltpu.VMEM((micro, rows, feats), jnp.bfloat16),
            pltpu.VMEM((micro, rows, feats), jnp.bfloat16),
            pltpu.VMEM((micro, rows, rows), jnp.bfloat16),
            pltpu.VMEM((64, feats), jnp.float32),
            pltpu.VMEM((REST, LANE), jnp.float32),
            pltpu.VMEM((rows, feats), jnp.bfloat16),
            pltpu.VMEM((64 * rows_in, rows), jnp.float32),
            pltpu.VMEM((64 * rows_out, rows), jnp.float32),
            dma,
            dma((micro,)),
            dma((2, 2, 4)),
            dma((2, 2, 4)),
            dma((2, 2)),
            dma((2, 2)),
            dma((8, 2, 2)),
            dma((8, 2, 2)),
            dma((8,)),
            dma((8,)),
            dma((micro,)),
            dma((micro,)),
        ],
        compiler_params=pltpu.CompilerParams(
            collective_id=0, has_side_effects=True, vmem_limit_bytes=60 * 1024 * 1024
        ),
    )(
        tokens_in[:, 0],
        keep_one[:, 0],
        keep_two[:, 0],
        keep_three[:, 0],
        norm_gain,
        layer_scale,
        w_qkv[0],
        w_out[0],
        jnp.asarray(every, jnp.bfloat16),
        jnp.asarray(rest, jnp.bfloat16),
    )
    return stash[None, :, None]


def solution(mesh):
    return jax.shard_map(
        shards,
        mesh=mesh,
        in_specs=(
            P(None, ("fsdp", "dp"), None, None),
            P(None, ("fsdp", "dp"), None),
            P(None, ("fsdp", "dp"), None),
            P(None, ("fsdp", "dp"), None),
            P("section", None),
            P("section", None),
            P("section", ("fsdp", "dp"), None),
            P("section", ("fsdp", "dp"), None),
        ),
        out_specs=P("section", None, ("fsdp", "dp"), None, None),
        check_vma=False,
    )
```

time: 577 us -> 172 us (0.30)
  waiting for transfers between devices: 413 us -> 0 us
  Pallas kernels: 0 us -> 168 us
  local copies, waits for them, and re-layouts: 59.6 us -> 2.77 us
  matrix products: 49.8 us -> 0 us
  other arithmetic: 24.8 us -> 0 us
  starting transfers between devices: 14.1 us -> 0 us
  between operations: 13.4 us -> 0.01 us
    ppermute x11 -> x0, waiting for transfers between devices: 222 us -> none  [shifted(): lax.ppermute(value, axis, [(source, source + steps) for source in range(f...]
    all_gather x2 -> x0, waiting for transfers between devices: 191 us -> none  [the longest x1 101 us: shards(): lax.all_gather(w_qkv, ('fsdp', 'dp'), axis=1, tiled=True)]
    pallas_call x0 -> x1, Pallas kernels: none -> 168 us  [shards(): pl.pallas_call(kernel, out_shape=jax.ShapeDtypeStruct((micro, rows, feats...]
    dot_general x16 -> x0, matrix products: 48 us -> none  [the longest x4 23.1 us: attend(): lax.dot_general(normed, proj_in, (((1,), (1,)), ((), ())), preferred_elem...]
    unnamed x8 -> x1, local copies, waits for them, and re-layouts: 19.6 us -> 2.77 us
    ppermute x11 -> x0, starting transfers between devices: 14.1 us -> none  [shifted(): lax.ppermute(value, axis, [(source, source + steps) for source in range(f...]
    dynamic_update_slice x11 -> x0, other arithmetic: 13.6 us -> none  [step(): lax.dynamic_update_index_in_dim(saved, jnp.where(active, result, before),...]
    dynamic_slice x12 -> x0, local copies, waits for them, and re-layouts: 12.7 us -> none  [the longest x11 11.5 us: step(): before = lax.dynamic_index_in_dim(saved, slot, 0, keepdims=False)]
  transfers between devices with their start and end apart: 13 -> 0, of which waited for: 13 -> 0; matrix products, arithmetic and copies ran while one was open for 6% -> 0% of each run, Pallas kernels for 0% -> 0%
where the time goes in v1:
time: 172 us; the launch traced here: 171 us
  Pallas kernels  168 us (98%)
  local copies, waits for them, and re-layouts  2.77 us (2%)
    pallas_call x1, Pallas kernels, shards(): pl.pallas_call(kernel, out_shape=jax.ShapeDtypeStruct((micro, rows, feats...  168 us

profile of v1, /device:TPU:56, one launch (start us, length us, event | category | flops | bytes accessed | tf_op | source)
XLA Modules:
  0.0 170.8 jit_solution(9838337440137885127)
XLA Ops:
  0.0 168.0 %shard_map.100 = bf16[4,128,1664]{2,1,0:T(8,128)(2,1)} custom-call(bf16[4,128,1664]{2,1,0:T(8,128)(2,1)} %bitcast.10, s32[4,96]{1,0:T(4,128)} %bitcast.13, s32[4,64]{1,0:T(4,128)} %bitcast.14, s32[4,48]{1,0:T(4,128)} %bitcast.15, f32[1,1664]{1,0:T(1,128)} %gain_ref.1, f32[1,1664]{1,0:T(1,128)} %scale_ref.1, bf16[39,1664]{1,0:T(8,128)(2,1)} %bitcast.11, ...), custom_call_target="tpu_custom_call" | custom-call | tf_op jit(solution)/shard_map/pallas_call | solution.py:437
  168.0 2.8 %copy.13 = bf16[1,4,1,128,1664]{4,3,2,1,0:T(8,128)(2,1)} copy(bf16[1,4,1,128,1664]{4,3,2,1,0:T(8,128)(2,1)} %bitcast.9) | data formatting | bytes 3407872

commit v2 on v1

--- a/solution.py
+++ b/solution.py
@@ -1,4 +1,4 @@
-import functools
+import heapq
 
 import jax
 import jax.numpy as jnp
@@ -17,6 +17,10 @@
 A_ROWS = 272
 A_HALF = 144
 B_HALF = 208
+TOTAL = 13 * MAIN + REST
+LAST = {"x": 2, "z": 4}
+SIGN = (-1, 1)
+FIRST = (("B", "z"), ("A", "x"), ("A", "z"), ("B", "x"))
 
 
 def compaction(rows_in, rows_out, tiles):
@@ -38,6 +42,50 @@
                 for tile in range(tiles):
                     rest[tile * 8 * left + place * left + i, place * REST + tile * left + i] = 1
     return every, rest
+
+
+def gather_plan():
+    size = {"A": A_ROWS * 512e-5, "B": (TOTAL - A_ROWS) * 512e-5}
+    queue, busy, seen, count, order = [], {}, {}, 0, []
+
+    def go(now, part, axis, d, k, other):
+        nonlocal count
+        length = size[part] * (0.5 if k == LAST[axis] else 1)
+        begin = max(now, busy.get((axis, d), 0.0))
+        busy[axis, d] = begin + length
+        count += 1
+        heapq.heappush(queue, (begin + length + 1.5, count, (part, axis, d, k, other)))
+
+    for part, axis in FIRST:
+        for d in range(2):
+            go(0.0, part, axis, d, 1, 0)
+    parts, packs = {}, []
+    while queue:
+        now, _, message = heapq.heappop(queue)
+        while packs and packs[0][0] <= now:
+            order.append(("pack", packs.pop(0)[1]))
+        order.append(message)
+        part, axis, d, k, other = message
+        if k < LAST[axis]:
+            go(now, part, axis, d, k + 1, other)
+        key = (part, axis, k if k == LAST[axis] else message, other)
+        seen[key] = seen.get(key, 0) + 1
+        if k == LAST[axis] and seen[key] < 2:
+            continue
+        away = LAST[axis] if k == LAST[axis] else SIGN[d] * k
+        turn = (part, axis) in (("A", "x"), ("B", "z"))
+        if turn:
+            for e in range(2):
+                go(now, part, "z" if axis == "x" else "x", e, 1, away)
+            order.append(("turn", part, away))
+        row = other if axis == "x" else away
+        if axis == "x" or part == "A":
+            parts[part, row] = parts.get((part, row), 0) + 1
+            if parts[part, row] == (3 if axis == "x" else 4):
+                order.append(("sib", part, row))
+                if parts.get(("B" if part == "A" else "A", row), 0) >= (3 if part == "B" and row == 0 else 4 if part == "B" else 3):
+                    packs.append((now + 2.5, row))
+    return order + [("pack", row) for _, row in packs]
 
 
 def kernel(
@@ -64,10 +112,15 @@
     normed,
     qkv,
     mixed,
+    every,
+    rest,
     tok_sem,
+    table_sem,
     out_sem,
-    z_send,
-    z_recv,
+    za_send,
+    za_recv,
+    zb_send,
+    zb_recv,
     xa_send,
     xa_recv,
     xb_send,
@@ -76,6 +129,8 @@
     sib_recv,
     t_send,
     t_recv,
+    ready,
+    turn,
 ):
     micro, rows, feats = tok_ref.shape
     tiles = feats // LANE
@@ -101,7 +156,6 @@
     sibling = (level, z, x * 2 + 1 - core)
     y_plus, y_minus = (lax.rem(level + 1, 8), z, dp), (lax.rem(level + 7, 8), z, dp)
 
-    recv[...] = jnp.zeros_like(recv)
     barrier = pltpu.get_barrier_semaphore()
     partners = (x_plus, x_minus, z_plus, z_minus, sibling, y_plus, y_minus)
     for partner in partners:
@@ -116,6 +170,12 @@
         small[tile * left : (tile + 1) * left, :] = stage[MAIN : MAIN + left, lanes]
     gbuf[core, z, x, tiles * MAIN : tiles * MAIN + REST, :] = small[...].astype(jnp.bfloat16)
 
+    tables = (
+        pltpu.make_async_copy(every_ref, every, table_sem.at[0]),
+        pltpu.make_async_copy(rest_ref, rest, table_sem.at[1]),
+    )
+    for table in tables:
+        table.start()
     pl.semaphore_wait(barrier, len(partners))
 
     total = tiles * MAIN + REST
@@ -140,59 +200,51 @@
             src_ref=part, dst_ref=part, send_sem=ss, recv_sem=rs, device_id=z_plus, device_id_type=MESH
         ).wait_recv()
 
-    zdir = (z_plus, z_minus)
-    xdir = (x_plus, x_minus)
-    sign = (-1, 1)
-
-    def at(dz, dx, part):
-        return gbuf.at[core, zat(dz), xat(dx), part]
-
-    def row(dz, part):
-        return gbuf.at[core, zat(dz), :, part]
-
-    def z_go(kind, d, k, part):
-        send(part, z_send.at[kind, d, k - 1], z_recv.at[kind, d, k - 1], zdir[d])
-
-    def z_come(kind, d, k, part):
-        arrive(part, z_send.at[kind, d, k - 1], z_recv.at[kind, d, k - 1])
-
-    def xa_go(d, k, part):
-        send(part, xa_send.at[d, k - 1], xa_recv.at[d, k - 1], xdir[d])
-
-    def xa_come(d, k, part):
-        arrive(part, xa_send.at[d, k - 1], xa_recv.at[d, k - 1])
-
-    def xb_go(dz, d, k, part):
-        i = dz % 8
-        send(part, xb_send.at[i, d, k - 1], xb_recv.at[i, d, k - 1], xdir[d])
-
-    def xb_come(dz, d, k, part):
-        i = dz % 8
-        arrive(part, xb_send.at[i, d, k - 1], xb_recv.at[i, d, k - 1])
-
-    def x_spread(dz):
-        for d in range(2):
-            xb_go(dz, d, 1, at(dz, 0, B))
-
-    def x_relay(dz):
-        for d in range(2):
-            xb_come(dz, d, 1, at(dz, sign[d], B))
-            xb_go(dz, d, 2, at(dz, sign[d], (B1, B2)[d]))
-
-    def x_end(dz):
-        for d in range(2):
-            xb_come(dz, d, 2, at(dz, 2 * sign[d], (B1, B2)[d]))
-
-    def to_sibling(dz):
-        i = dz % 8
-        send(gbuf.at[core, zat(dz)], sib_send.at[i], sib_recv.at[i], sibling)
+    targets = {"x": (x_plus, x_minus), "z": (z_plus, z_minus)}
+    rows_of = {"A": (A, A1, A2), "B": (B, B1, B2)}
+
+    def at(dz, dx, piece):
+        return gbuf.at[core, zat(dz), xat(dx), piece]
+
+    def lane_of(message):
+        part, axis, d, k, other = message
+        piece = rows_of[part][1 + d if k == LAST[axis] else 0]
+        away = SIGN[d] * k
+        place = at(other, away, piece) if axis == "x" else at(away, other, piece)
+        if axis == "z" and part == "A":
+            index = (d, k - 1, other % 4)
+            return place, za_send.at[index], za_recv.at[index]
+        if axis == "z":
+            return place, zb_send.at[d, k - 1], zb_recv.at[d, k - 1]
+        if part == "A":
+            return place, xa_send.at[d, k - 1], xa_recv.at[d, k - 1]
+        index = (other % 8, d, k - 1)
+        return place, xb_send.at[index], xb_recv.at[index]
+
+    def post(part, axis, d, k, other):
+        piece = rows_of[part][1 + d if k == LAST[axis] else 0]
+        away = SIGN[d] * (k - 1)
+        place = at(other, away, piece) if axis == "x" else at(away, other, piece)
+        _, ss, rs = lane_of((part, axis, d, k, other))
+        send(place, ss, rs, targets[axis][d])
+
+    def take(message):
+        part, axis, d, k, other = message
+        arrive(*lane_of(message))
+        if k < LAST[axis]:
+            post(part, axis, d, k + 1, other)
+
+    def to_sibling(part, dz):
+        i = (dz % 8, "AB".index(part))
+        send(gbuf.at[core, zat(dz), :, rows_of[part][0]], sib_send.at[i], sib_recv.at[i], sibling)
 
     def pack(dz):
-        i = dz % 8
         g = zat(dz)
-        arrive(gbuf.at[1 - core, g], sib_send.at[i], sib_recv.at[i])
+        for i, part in enumerate("AB"):
+            index = (dz % 8, i)
+            arrive(gbuf.at[1 - core, g, :, rows_of[part][0]], sib_send.at[index], sib_recv.at[index])
         tail = gbuf[:, g, :, tiles * MAIN : tiles * MAIN + REST, :].reshape(8 * REST, LANE)
-        tail = jnp.dot(rest_ref[...], tail, preferred_element_type=jnp.float32).astype(jnp.bfloat16)
+        tail = jnp.dot(rest[...], tail, preferred_element_type=jnp.float32).astype(jnp.bfloat16)
         for tile in range(0, tiles, 2):
             count = min(2, tiles - tile)
             columns = [
@@ -206,17 +258,21 @@
                 for t in range(tile, tile + count)
             ]
             block = columns[0] if count == 1 else jnp.concatenate(columns, axis=1)
-            dense = jnp.dot(every_ref[...], block, preferred_element_type=jnp.float32).astype(jnp.bfloat16)
+            dense = jnp.dot(every[...], block, preferred_element_type=jnp.float32).astype(jnp.bfloat16)
             lanes = slice(tile * LANE, (tile + count) * LANE)
             pad_in = wd.shape[1]
             wd[g, :, lanes] = dense[:pad_in]
             wod[g, :, lanes] = dense[pad_in:]
 
-    for d in range(2):
-        z_go(1, d, 1, at(0, 0, B))
-    for d in range(2):
-        xa_go(d, 1, at(0, 0, A))
-    x_spread(0)
+    for part, axis in FIRST:
+        for d in range(2):
+            post(part, axis, d, 1, 0)
+
+    recv[...] = jnp.zeros_like(recv)
+
+    @pl.when(level > 0)
+    def _():
+        pl.semaphore_signal(ready, inc=1, device_id=y_minus, device_id_type=MESH)
 
     @pl.when(level == 0)
     def _():
@@ -233,83 +289,29 @@
                 hit = place == chosen[m : m + 1, :]
                 picks[m, :, 0:count] = jnp.where(hit, 1.0, 0.0).astype(jnp.bfloat16)
 
-    for d in range(2):
-        xa_come(d, 1, at(0, sign[d], A))
-        xa_go(d, 2, at(0, sign[d], (A1, A2)[d]))
-
-    def z_relay(k):
-        for d in range(2):
-            if k < 4:
-                z_come(1, d, k, at(sign[d] * k, 0, B))
-                z_go(1, d, k + 1, at(sign[d] * k, 0, B if k < 3 else (B1, B2)[d]))
-                x_spread(sign[d] * k)
-            else:
-                z_come(1, d, k, at(4, 0, (B1, B2)[d]))
-        if k == 4:
-            x_spread(4)
-
-    def za_relay(k):
-        for d in range(2):
-            if k < 4:
-                z_come(0, d, k, row(sign[d] * k, A))
-                z_go(0, d, k + 1, row(sign[d] * k, A if k < 3 else (A1, A2)[d]))
-            else:
-                z_come(0, d, k, row(4, (A1, A2)[d]))
-
-    z_relay(1)
-    x_relay(0)
-    for d in range(2):
-        xa_come(d, 2, at(0, 2, (A1, A2)[d]))
-    for d in range(2):
-        z_go(0, d, 1, row(0, A))
-    z_relay(2)
-    x_relay(-1)
-    x_relay(1)
-    z_relay(3)
-    za_relay(1)
-    x_relay(-2)
-    x_relay(2)
-    z_relay(4)
-    x_end(0)
-    to_sibling(0)
-    za_relay(2)
-    x_relay(-3)
-    x_relay(3)
-    x_end(-1)
-    x_end(1)
-    to_sibling(-1)
-    to_sibling(1)
-    pack(0)
-    za_relay(3)
-    x_relay(4)
-    x_end(-2)
-    x_end(2)
-    to_sibling(-2)
-    to_sibling(2)
-    pack(-1)
-    pack(1)
-    x_end(-3)
-    x_end(3)
-    to_sibling(-3)
-    to_sibling(3)
-    pack(-2)
-    pack(2)
-    za_relay(4)
-    x_end(4)
-    to_sibling(4)
-    pack(-3)
-    pack(3)
-    pack(4)
+    for table in tables:
+        table.wait()
+    for event in gather_plan():
+        if event[0] == "sib":
+            to_sibling(*event[1:])
+        elif event[0] == "pack":
+            pack(event[1])
+        elif event[0] == "turn":
+            for d in range(2):
+                post(event[1], "z" if event[1] == "A" else "x", d, 1, event[2])
+        else:
+            take(event)
 
     live = rows - 32 * (level >= 2).astype(jnp.int32)
     live = live - 32 * (level >= 4).astype(jnp.int32) - 16 * (level >= 6).astype(jnp.int32)
 
-    def token_copy(m, source, count):
+    def token_copy(m, source, count, low=0):
+        i = 1 if low else 0
         return pltpu.make_async_remote_copy(
-            src_ref=source.at[m, pl.ds(0, count)],
-            dst_ref=recv.at[m, pl.ds(0, count)],
-            send_sem=t_send.at[m],
-            recv_sem=t_recv.at[m],
+            src_ref=source.at[m, pl.ds(low, count)],
+            dst_ref=recv.at[m, pl.ds(low, count)],
+            send_sem=t_send.at[i, m],
+            recv_sem=t_recv.at[i, m],
             device_id=y_plus,
             device_id_type=MESH,
         )
@@ -319,9 +321,15 @@
         pltpu.make_async_copy(tok_ref, recv, tok_sem).wait()
 
     counts = (one_ref.shape[1], two_ref.shape[1], three_ref.shape[1])
-    incoming = ((1, 1, rows), (2, 3, counts[0]), (4, 5, counts[1]), (6, 7, counts[2]))
+    incoming = ((2, 3, counts[0]), (4, 5, counts[1]), (6, 7, counts[2]))
+    early = 3 * rows // 4
 
     def body(m, carry):
+        @pl.when(level == 1)
+        def _():
+            token_copy(m, recv, early).wait_recv()
+            token_copy(m, recv, rows - early, early).wait_recv()
+
         for low, high, count in incoming:
 
             @pl.when(jnp.logical_and(level >= low, level <= high))
@@ -333,15 +341,23 @@
         spread = jnp.mean(center * center, axis=-1, keepdims=True)
         normed[...] = (center * lax.rsqrt(spread + EPS) * gain_ref[...]).astype(jnp.bfloat16)
 
-        def project(g, carry):
+        every_row = wd.reshape(8 * wd.shape[1], feats)
+        half = 4 * wd.shape[1]
+
+        def project(i, carry):
             part = lax.dot_general(
-                wd[g], normed[...], (((1,), (1,)), ((), ())), preferred_element_type=jnp.float32
+                every_row[pl.ds(pl.multiple_of(i * half, 16), half), :],
+                normed[...],
+                (((1,), (1,)), ((), ())),
+                preferred_element_type=jnp.float32,
             )
-            start = pl.multiple_of(g * group_in, 8)
-            qkv[pl.ds(start, group_in), :] = part[:group_in]
+            for g in range(4):
+                low = g * wd.shape[1]
+                start = pl.multiple_of((i * 4 + g) * group_in, 8)
+                qkv[pl.ds(start, group_in), :] = part[low : low + group_in]
             return carry
 
-        lax.fori_loop(0, 8, project, 0)
+        lax.fori_loop(0, 2, project, 0)
 
         inside = lax.broadcasted_iota(jnp.int32, (rows, rows), 0) < live
         for h in range(heads):
@@ -355,7 +371,7 @@
             scores = jnp.where(inside, scores, -1e30)
             top = jnp.max(scores, axis=0, keepdims=True)
             expo = jnp.exp(scores - top)
-            weights = (expo / jnp.sum(expo, axis=0, keepdims=True)).astype(jnp.bfloat16)
+            weights = (expo * (1.0 / jnp.sum(expo, axis=0, keepdims=True))).astype(jnp.bfloat16)
             mixed[low : low + HDIM, :] = jnp.dot(vals, weights, preferred_element_type=jnp.float32)
 
         parts = []
@@ -377,26 +393,44 @@
 
         pltpu.make_async_copy(res.at[m], out_ref.at[m], out_sem.at[m]).start()
 
-        for here, count in ((0, rows), (2, counts[0]), (4, counts[1]), (6, counts[2])):
+        @pl.when(jnp.logical_and(m == 0, level < 7))
+        def _():
+            pl.semaphore_wait(ready, 1)
+
+        @pl.when(level == 0)
+        def _():
+            @pl.when(jnp.logical_or(m > 0, core == 1))
+            def _():
+                pl.semaphore_wait(turn, 1)
+
+            token_copy(m, res, early).start()
+            token_copy(m, res, rows - early, early).start()
+            token_copy(m, res, early).wait_send()
+
+            @pl.when(jnp.logical_or(m < micro - 1, core == 0))
+            def _():
+                pl.semaphore_signal(turn, inc=1, device_id=sibling, device_id_type=MESH)
+
+        for here, count in ((2, counts[0]), (4, counts[1]), (6, counts[2])):
 
             @pl.when(level == here)
             def _():
                 token_copy(m, res, count).start()
 
+        @pl.when(jnp.logical_and(lax.rem(level, 2) == 1, level < 7))
+        def _():
+            for low in range(0, feats, 4 * LANE):
+                size = min(4 * LANE, feats - low)
+                lanes = slice(low, low + size)
+                taken = lax.dot_general(
+                    picks[m], res[m, :, lanes], (((0,), (0,)), ((), ())), preferred_element_type=jnp.float32
+                )
+                pruned[m, :, lanes] = taken.astype(jnp.bfloat16)
+
         for here, count in ((1, counts[0]), (3, counts[1]), (5, counts[2])):
 
             @pl.when(level == here)
             def _():
-                for low in range(0, feats, 4 * LANE):
-                    size = min(4 * LANE, feats - low)
-                    lanes = slice(low, low + size)
-                    taken = lax.dot_general(
-                        picks[m],
-                        res[m, :, lanes],
-                        (((0,), (0,)), ((), ())),
-                        preferred_element_type=jnp.float32,
-                    )
-                    pruned[m, :, lanes] = taken.astype(jnp.bfloat16)
                 token_copy(m, pruned, count).start()
 
         return carry
@@ -408,7 +442,11 @@
 
     def finish(m, carry):
         pltpu.make_async_copy(res.at[m], out_ref.at[m], out_sem.at[m]).wait()
-        for here, count in ((0, rows), (2, counts[0]), (4, counts[1]), (6, counts[2])):
+        @pl.when(level == 0)
+        def _():
+            token_copy(m, res, rows - early, early).wait_send()
+
+        for here, count in ((2, counts[0]), (4, counts[1]), (6, counts[2])):
 
             @pl.when(level == here)
             def _():
@@ -437,7 +475,7 @@
     stash = pl.pallas_call(
         kernel,
         out_shape=jax.ShapeDtypeStruct((micro, rows, feats), jnp.bfloat16),
-        in_specs=[pl.BlockSpec(memory_space=pl.ANY)] + [vmem] * 9,
+        in_specs=[pl.BlockSpec(memory_space=pl.ANY)] + [vmem] * 7 + [pl.BlockSpec(memory_space=pl.ANY)] * 2,
         out_specs=pl.BlockSpec(memory_space=pl.ANY),
         scratch_shapes=[
             pltpu.VMEM((2, 8, 4, tiles * MAIN + REST, LANE), jnp.bfloat16),
@@ -452,18 +490,25 @@
             pltpu.VMEM((rows, feats), jnp.bfloat16),
             pltpu.VMEM((64 * rows_in, rows), jnp.float32),
             pltpu.VMEM((64 * rows_out, rows), jnp.float32),
+            pltpu.VMEM(every.shape, jnp.bfloat16),
+            pltpu.VMEM(rest.shape, jnp.bfloat16),
             dma,
+            dma((2,)),
             dma((micro,)),
-            dma((2, 2, 4)),
-            dma((2, 2, 4)),
+            dma((2, 4, 4)),
+            dma((2, 4, 4)),
+            dma((2, 4)),
+            dma((2, 4)),
             dma((2, 2)),
             dma((2, 2)),
             dma((8, 2, 2)),
             dma((8, 2, 2)),
-            dma((8,)),
-            dma((8,)),
-            dma((micro,)),
-            dma((micro,)),
+            dma((8, 2)),
+            dma((8, 2)),
+            dma((2, micro)),
+            dma((2, micro)),
+            pltpu.SemaphoreType.REGULAR,
+            pltpu.SemaphoreType.REGULAR,
         ],
         compiler_params=pltpu.CompilerParams(
             collective_id=0, has_side_effects=True, vmem_limit_bytes=60 * 1024 * 1024

time: 172 us -> 160 us (0.930)
  Pallas kernels: 168 us -> 157 us
    pallas_call x1, Pallas kernels: 168 us -> 157 us  [shards(): pl.pallas_call(kernel, out_shape=jax.ShapeDtypeStruct((micro, rows, feats...]
where the time goes in v2:
time: 160 us
  Pallas kernels  157 us (98%)
  local copies, waits for them, and re-layouts  2.77 us (2%)
    pallas_call x1, Pallas kernels, shards(): pl.pallas_call(kernel, out_shape=jax.ShapeDtypeStruct((micro, rows, feats...  157 us

profile of v2, /device:TPU:56, one launch (start us, length us, event | category | flops | bytes accessed | tf_op | source)
XLA Modules:
  0.0 160.1 jit_solution(7634438572479182108)
XLA Ops:
  0.0 157.3 %shard_map.100 = bf16[4,128,1664]{2,1,0:T(8,128)(2,1)} custom-call(bf16[4,128,1664]{2,1,0:T(8,128)(2,1)} %bitcast.10, s32[4,96]{1,0:T(4,128)} %bitcast.13, s32[4,64]{1,0:T(4,128)} %bitcast.14, s32[4,48]{1,0:T(4,128)} %bitcast.15, f32[1,1664]{1,0:T(1,128)} %gain_ref.1, f32[1,1664]{1,0:T(1,128)} %scale_ref.1, bf16[39,1664]{1,0:T(8,128)(2,1)} %bitcast.11, ...), custom_call_target="tpu_custom_call" | custom-call | tf_op jit(solution)/shard_map/pallas_call | solution.py:475
  157.3 2.8 %copy.13 = bf16[1,4,1,128,1664]{4,3,2,1,0:T(8,128)(2,1)} copy(bf16[1,4,1,128,1664]{4,3,2,1,0:T(8,128)(2,1)} %bitcast.9) | data formatting | bytes 3407872

commit v3 on v2

--- a/solution.py
+++ b/solution.py
@@ -20,6 +20,7 @@
 TOTAL = 13 * MAIN + REST
 LAST = {"x": 2, "z": 4}
 SIGN = (-1, 1)
+CUTS = (0, 768, 1280, 1664)
 FIRST = (("B", "z"), ("A", "x"), ("A", "z"), ("B", "x"))
 
 
@@ -114,6 +115,9 @@
     mixed,
     every,
     rest,
+    partial,
+    stat_in,
+    stat_out,
     tok_sem,
     table_sem,
     out_sem,
@@ -305,59 +309,85 @@
     live = rows - 32 * (level >= 2).astype(jnp.int32)
     live = live - 32 * (level >= 4).astype(jnp.int32) - 16 * (level >= 6).astype(jnp.int32)
 
-    def token_copy(m, source, count, low=0):
-        i = 1 if low else 0
+    def token_copy(i, m, source, count):
+        if i == 3:
+            src, dst = stat_out.at[m], stat_in.at[m]
+        else:
+            lanes = pl.ds(CUTS[i], CUTS[i + 1] - CUTS[i])
+            src, dst = source.at[m, pl.ds(0, count), lanes], recv.at[m, pl.ds(0, count), lanes]
         return pltpu.make_async_remote_copy(
-            src_ref=source.at[m, pl.ds(low, count)],
-            dst_ref=recv.at[m, pl.ds(low, count)],
+            src_ref=src,
+            dst_ref=dst,
             send_sem=t_send.at[i, m],
             recv_sem=t_recv.at[i, m],
             device_id=y_plus,
             device_id_type=MESH,
         )
 
+    def row_stats(values):
+        values = values.astype(jnp.float32)
+        mean = jnp.mean(values, axis=-1, keepdims=True)
+        center = values - mean
+        spread = lax.rsqrt(jnp.mean(center * center, axis=-1, keepdims=True) + EPS)
+        column = lax.broadcasted_iota(jnp.int32, (rows, LANE), 1)
+        both = jnp.where(column == 0, mean, jnp.where(column == 1, spread, 0.0))
+        return jnp.transpose(both)[:8]
+
     @pl.when(level == 0)
     def _():
         pltpu.make_async_copy(tok_ref, recv, tok_sem).wait()
 
+        def prepare(m, carry):
+            stat_in[m] = row_stats(recv[m])
+            return carry
+
+        lax.fori_loop(0, micro, prepare, 0)
+
     counts = (one_ref.shape[1], two_ref.shape[1], three_ref.shape[1])
-    incoming = ((2, 3, counts[0]), (4, 5, counts[1]), (6, 7, counts[2]))
-    early = 3 * rows // 4
+    incoming = ((1, 1, rows), (2, 3, counts[0]), (4, 5, counts[1]), (6, 7, counts[2]))
+    outgoing = ((2, res, counts[0]), (4, res, counts[1]), (6, res, counts[2]))
+    outgoing += ((1, pruned, counts[0]), (3, pruned, counts[1]), (5, pruned, counts[2]))
+    order = (3, 0, 1, 2)
 
     def body(m, carry):
-        @pl.when(level == 1)
-        def _():
-            token_copy(m, recv, early).wait_recv()
-            token_copy(m, recv, rows - early, early).wait_recv()
-
-        for low, high, count in incoming:
-
-            @pl.when(jnp.logical_and(level >= low, level <= high))
-            def _():
-                token_copy(m, recv, count).wait_recv()
-
-        values = recv[m].astype(jnp.float32)
-        center = values - jnp.mean(values, axis=-1, keepdims=True)
-        spread = jnp.mean(center * center, axis=-1, keepdims=True)
-        normed[...] = (center * lax.rsqrt(spread + EPS) * gain_ref[...]).astype(jnp.bfloat16)
-
+        def await_tokens(i):
+            for low, high, count in incoming:
+
+                @pl.when(jnp.logical_and(level >= low, level <= high))
+                def _():
+                    token_copy(i, m, recv, count).wait_recv()
+
+        await_tokens(3)
+        columns = jnp.transpose(jnp.concatenate([stat_in[m], jnp.zeros((LANE - 8, rows), jnp.float32)], axis=0))
+        mean, spread = columns[:, 0:1], columns[:, 1:2]
         every_row = wd.reshape(8 * wd.shape[1], feats)
         half = 4 * wd.shape[1]
-
-        def project(i, carry):
-            part = lax.dot_general(
-                every_row[pl.ds(pl.multiple_of(i * half, 16), half), :],
-                normed[...],
-                (((1,), (1,)), ((), ())),
-                preferred_element_type=jnp.float32,
-            )
-            for g in range(4):
-                low = g * wd.shape[1]
-                start = pl.multiple_of((i * 4 + g) * group_in, 8)
-                qkv[pl.ds(start, group_in), :] = part[low : low + group_in]
-            return carry
-
-        lax.fori_loop(0, 2, project, 0)
+        for i in range(3):
+            lanes = slice(CUTS[i], CUTS[i + 1])
+            await_tokens(i)
+            center = recv[m, :, lanes].astype(jnp.float32) - mean
+            normed[:, lanes] = (center * spread * gain_ref[:, lanes]).astype(jnp.bfloat16)
+
+            def project(j, carry):
+                these = pl.ds(pl.multiple_of(j * half, 16), half)
+                part = lax.dot_general(
+                    every_row[these, lanes],
+                    normed[:, lanes],
+                    (((1,), (1,)), ((), ())),
+                    preferred_element_type=jnp.float32,
+                )
+                if i > 0:
+                    part = part + partial[these, :]
+                if i < 2:
+                    partial[these, :] = part
+                else:
+                    for g in range(4):
+                        low = g * wd.shape[1]
+                        start = pl.multiple_of((j * 4 + g) * group_in, 8)
+                        qkv[pl.ds(start, group_in), :] = part[low : low + group_in]
+                return carry
+
+            lax.fori_loop(0, 2, project, 0)
 
         inside = lax.broadcasted_iota(jnp.int32, (rows, rows), 0) < live
         for h in range(heads):
@@ -397,25 +427,23 @@
         def _():
             pl.semaphore_wait(ready, 1)
 
+        @pl.when(lax.rem(level, 2) == 0)
+        def _():
+            stat_out[m] = row_stats(res[m])
+
         @pl.when(level == 0)
         def _():
             @pl.when(jnp.logical_or(m > 0, core == 1))
             def _():
                 pl.semaphore_wait(turn, 1)
 
-            token_copy(m, res, early).start()
-            token_copy(m, res, rows - early, early).start()
-            token_copy(m, res, early).wait_send()
+            for i in order:
+                token_copy(i, m, res, rows).start()
+            token_copy(1, m, res, rows).wait_send()
 
             @pl.when(jnp.logical_or(m < micro - 1, core == 0))
             def _():
                 pl.semaphore_signal(turn, inc=1, device_id=sibling, device_id_type=MESH)
-
-        for here, count in ((2, counts[0]), (4, counts[1]), (6, counts[2])):
-
-            @pl.when(level == here)
-            def _():
-                token_copy(m, res, count).start()
 
         @pl.when(jnp.logical_and(lax.rem(level, 2) == 1, level < 7))
         def _():
@@ -426,12 +454,14 @@
                     picks[m], res[m, :, lanes], (((0,), (0,)), ((), ())), preferred_element_type=jnp.float32
                 )
                 pruned[m, :, lanes] = taken.astype(jnp.bfloat16)
-
-        for here, count in ((1, counts[0]), (3, counts[1]), (5, counts[2])):
+            stat_out[m] = row_stats(pruned[m])
+
+        for here, source, count in outgoing:
 
             @pl.when(level == here)
             def _():
-                token_copy(m, pruned, count).start()
+                for i in order:
+                    token_copy(i, m, source, count).start()
 
         return carry
 
@@ -444,19 +474,15 @@
         pltpu.make_async_copy(res.at[m], out_ref.at[m], out_sem.at[m]).wait()
         @pl.when(level == 0)
         def _():
-            token_copy(m, res, rows - early, early).wait_send()
-
-        for here, count in ((2, counts[0]), (4, counts[1]), (6, counts[2])):
+            for i in (3, 0, 2):
+                token_copy(i, m, res, rows).wait_send()
+
+        for here, source, count in outgoing:
 
             @pl.when(level == here)
             def _():
-                token_copy(m, res, count).wait_send()
-
-        for here, count in ((1, counts[0]), (3, counts[1]), (5, counts[2])):
-
-            @pl.when(level == here)
-            def _():
-                token_copy(m, pruned, count).wait_send()
+                for i in order:
+                    token_copy(i, m, source, count).wait_send()
 
         return carry
 
@@ -492,6 +518,9 @@
             pltpu.VMEM((64 * rows_out, rows), jnp.float32),
             pltpu.VMEM(every.shape, jnp.bfloat16),
             pltpu.VMEM(rest.shape, jnp.bfloat16),
+            pltpu.VMEM((8 * pad_in, rows), jnp.float32),
+            pltpu.VMEM((micro, 8, rows), jnp.float32),
+            pltpu.VMEM((micro, 8, rows), jnp.float32),
             dma,
             dma((2,)),
             dma((micro,)),
@@ -505,8 +534,8 @@
             dma((8, 2, 2)),
             dma((8, 2)),
             dma((8, 2)),
-            dma((2, micro)),
-            dma((2, micro)),
+            dma((4, micro)),
+            dma((4, micro)),
             pltpu.SemaphoreType.REGULAR,
             pltpu.SemaphoreType.REGULAR,
         ],

time: 160 us -> 157 us (0.981); the launches traced: 160 us -> 154 us
  Pallas kernels: 157 us -> 152 us
    pallas_call x1, Pallas kernels: 157 us -> 152 us  [shards(): pl.pallas_call(kernel, out_shape=jax.ShapeDtypeStruct((micro, rows, feats...]
where the time goes in v3:
time: 157 us; the launch traced here: 154 us
  Pallas kernels  152 us (97%)
  local copies, waits for them, and re-layouts  2.77 us (2%)
    pallas_call x1, Pallas kernels, shards(): pl.pallas_call(kernel, out_shape=jax.ShapeDtypeStruct((micro, rows, feats...  152 us

profile of v3, /device:TPU:56, one launch (start us, length us, event | category | flops | bytes accessed | tf_op | source)
XLA Modules:
  0.0 154.4 jit_solution(2784195431575997227)
XLA Ops:
  0.0 151.7 %shard_map.100 = bf16[4,128,1664]{2,1,0:T(8,128)(2,1)} custom-call(bf16[4,128,1664]{2,1,0:T(8,128)(2,1)} %bitcast.10, s32[4,96]{1,0:T(4,128)} %bitcast.13, s32[4,64]{1,0:T(4,128)} %bitcast.14, s32[4,48]{1,0:T(4,128)} %bitcast.15, f32[1,1664]{1,0:T(1,128)} %gain_ref.1, f32[1,1664]{1,0:T(1,128)} %scale_ref.1, bf16[39,1664]{1,0:T(8,128)(2,1)} %bitcast.11, ...), custom_call_target="tpu_custom_call" | custom-call | tf_op jit(solution)/shard_map/pallas_call | solution.py:501
  151.7 2.8 %copy.13 = bf16[1,4,1,128,1664]{4,3,2,1,0:T(8,128)(2,1)} copy(bf16[1,4,1,128,1664]{4,3,2,1,0:T(8,128)(2,1)} %bitcast.9) | data formatting | bytes 3407872

commit v4 on v3

--- a/solution.py
+++ b/solution.py
@@ -21,6 +21,7 @@
 LAST = {"x": 2, "z": 4}
 SIGN = (-1, 1)
 CUTS = (0, 768, 1280, 1664)
+AHEAD = 1
 FIRST = (("B", "z"), ("A", "x"), ("A", "z"), ("B", "x"))
 
 
@@ -111,6 +112,7 @@
     stage,
     small,
     normed,
+    ahead,
     qkv,
     mixed,
     every,
@@ -268,6 +270,15 @@
             wd[g, :, lanes] = dense[:pad_in]
             wod[g, :, lanes] = dense[pad_in:]
 
+        @pl.when(level == 0)
+        def _():
+            part = lax.dot_general(
+                wd[g], ahead[...], (((1,), (1,)), ((), ())), preferred_element_type=jnp.float32
+            )
+            start = pl.multiple_of(g * group_in, 8)
+            for m in range(AHEAD):
+                qkv[m, pl.ds(start, group_in), :] = part[:group_in, m * rows : (m + 1) * rows]
+
     for part, axis in FIRST:
         for d in range(2):
             post(part, axis, d, 1, 0)
@@ -293,9 +304,28 @@
                 hit = place == chosen[m : m + 1, :]
                 picks[m, :, 0:count] = jnp.where(hit, 1.0, 0.0).astype(jnp.bfloat16)
 
+    def norm_ahead():
+        @pl.when(level == 0)
+        def _():
+            pltpu.make_async_copy(tok_ref, recv, tok_sem).wait()
+
+            def norm(m, carry):
+                values = recv[m].astype(jnp.float32)
+                center = values - jnp.mean(values, axis=-1, keepdims=True)
+                spread = lax.rsqrt(jnp.mean(center * center, axis=-1, keepdims=True) + EPS)
+                result = (center * spread * gain_ref[...]).astype(jnp.bfloat16)
+                ahead[pl.ds(pl.multiple_of(m * rows, rows), rows), :] = result
+                return carry
+
+            lax.fori_loop(0, AHEAD, norm, 0)
+
     for table in tables:
         table.wait()
-    for event in gather_plan():
+    plan = gather_plan()
+    first_pack = [event[0] for event in plan].index("pack")
+    for i, event in enumerate(plan):
+        if i == first_pack:
+            norm_ahead()
         if event[0] == "sib":
             to_sibling(*event[1:])
         elif event[0] == "pack":
@@ -333,16 +363,6 @@
         both = jnp.where(column == 0, mean, jnp.where(column == 1, spread, 0.0))
         return jnp.transpose(both)[:8]
 
-    @pl.when(level == 0)
-    def _():
-        pltpu.make_async_copy(tok_ref, recv, tok_sem).wait()
-
-        def prepare(m, carry):
-            stat_in[m] = row_stats(recv[m])
-            return carry
-
-        lax.fori_loop(0, micro, prepare, 0)
-
     counts = (one_ref.shape[1], two_ref.shape[1], three_ref.shape[1])
     incoming = ((1, 1, rows), (2, 3, counts[0]), (4, 5, counts[1]), (6, 7, counts[2]))
     outgoing = ((2, res, counts[0]), (4, res, counts[1]), (6, res, counts[2]))
@@ -350,6 +370,7 @@
     order = (3, 0, 1, 2)
 
     def body(m, carry):
+        slot = lax.rem(m, AHEAD)
         def await_tokens(i):
             for low, high, count in incoming:
 
@@ -357,44 +378,59 @@
                 def _():
                     token_copy(i, m, recv, count).wait_recv()
 
-        await_tokens(3)
-        columns = jnp.transpose(jnp.concatenate([stat_in[m], jnp.zeros((LANE - 8, rows), jnp.float32)], axis=0))
-        mean, spread = columns[:, 0:1], columns[:, 1:2]
-        every_row = wd.reshape(8 * wd.shape[1], feats)
-        half = 4 * wd.shape[1]
-        for i in range(3):
-            lanes = slice(CUTS[i], CUTS[i + 1])
-            await_tokens(i)
-            center = recv[m, :, lanes].astype(jnp.float32) - mean
-            normed[:, lanes] = (center * spread * gain_ref[:, lanes]).astype(jnp.bfloat16)
-
-            def project(j, carry):
-                these = pl.ds(pl.multiple_of(j * half, 16), half)
-                part = lax.dot_general(
-                    every_row[these, lanes],
-                    normed[:, lanes],
-                    (((1,), (1,)), ((), ())),
-                    preferred_element_type=jnp.float32,
-                )
-                if i > 0:
-                    part = part + partial[these, :]
-                if i < 2:
-                    partial[these, :] = part
-                else:
-                    for g in range(4):
-                        low = g * wd.shape[1]
-                        start = pl.multiple_of((j * 4 + g) * group_in, 8)
-                        qkv[pl.ds(start, group_in), :] = part[low : low + group_in]
-                return carry
-
-            lax.fori_loop(0, 2, project, 0)
+        @pl.when(jnp.logical_and(m == 0, level < 7))
+        def _():
+            pl.semaphore_wait(ready, 1)
+
+        @pl.when(jnp.logical_or(level > 0, m >= AHEAD))
+        def _():
+            @pl.when(jnp.logical_and(level == 0, m >= AHEAD))
+            def _():
+                stat_in[m] = row_stats(recv[m])
+
+            await_tokens(3)
+            columns = jnp.transpose(jnp.concatenate([stat_in[m], jnp.zeros((LANE - 8, rows), jnp.float32)], axis=0))
+            mean, spread = columns[:, 0:1], columns[:, 1:2]
+            every_row = wd.reshape(8 * wd.shape[1], feats)
+            half = 4 * wd.shape[1]
+            for i in range(3):
+                lanes = slice(CUTS[i], CUTS[i + 1])
+                await_tokens(i)
+                center = recv[m, :, lanes].astype(jnp.float32) - mean
+                normed[:, lanes] = (center * spread * gain_ref[:, lanes]).astype(jnp.bfloat16)
+
+                def project(j, carry):
+                    these = pl.ds(pl.multiple_of(j * half, 16), half)
+                    part = lax.dot_general(
+                        every_row[these, lanes],
+                        normed[:, lanes],
+                        (((1,), (1,)), ((), ())),
+                        preferred_element_type=jnp.float32,
+                    )
+                    if i > 0:
+                        part = part + partial[these, :]
+                    if i < 2:
+                        partial[these, :] = part
+                    else:
+                        for g in range(4):
+                            low = g * wd.shape[1]
+                            start = pl.multiple_of((j * 4 + g) * group_in, 8)
+                            qkv[slot, pl.ds(start, group_in), :] = part[low : low + group_in]
+                    return carry
+
+                lax.fori_loop(0, 2, project, 0)
+
+        @pl.when(jnp.logical_and(level == 0, m > 0))
+        def _():
+            token_copy(1, m - 1, res, rows).wait_send()
+            pl.semaphore_signal(turn, inc=1, device_id=sibling, device_id_type=MESH)
 
         inside = lax.broadcasted_iota(jnp.int32, (rows, rows), 0) < live
         for h in range(heads):
             low = h * HDIM
-            query = (qkv[low : low + HDIM, :].astype(jnp.bfloat16) * jnp.bfloat16(HDIM**-0.5))
-            keys = qkv[width + low : width + low + HDIM, :].astype(jnp.bfloat16)
-            vals = qkv[2 * width + low : 2 * width + low + HDIM, :].astype(jnp.bfloat16)
+            query = (qkv[slot, low : low + HDIM, :].astype(jnp.bfloat16) * jnp.bfloat16(HDIM**-0.5))
+            keys = qkv[slot, width + low : width + low + HDIM, :].astype(jnp.bfloat16)
+            vals = qkv[slot, 2 * width + low : 2 * width + low + HDIM, :].astype(jnp.bfloat16)
             scores = lax.dot_general(
                 keys, query, (((0,), (0,)), ((), ())), preferred_element_type=jnp.float32
             )
@@ -412,56 +448,58 @@
                 parts.append(gap)
         across = jnp.transpose(jnp.concatenate(parts, axis=0)).astype(jnp.bfloat16)
         alive = lax.broadcasted_iota(jnp.int32, (rows, LANE), 0) < live
-        for low in range(0, feats, 4 * LANE):
-            size = min(4 * LANE, feats - low)
-            lanes = slice(low, low + size)
-            block = wod[:, :, lanes].reshape(8 * wod.shape[1], size)
+        prunes = jnp.logical_and(lax.rem(level, 2) == 1, level < 7)
+
+        def start(which):
+            for here, source, count in outgoing:
+
+                @pl.when(level == here)
+                def _():
+                    for i in which:
+                        token_copy(i, m, source, count).start()
+
+        for i in range(3):
+            lanes = slice(CUTS[i], CUTS[i + 1])
+            block = wod[:, :, lanes].reshape(8 * wod.shape[1], CUTS[i + 1] - CUTS[i])
             branch = jnp.dot(across, block, preferred_element_type=jnp.float32)
             sums = recv[m, :, lanes].astype(jnp.float32) + scale_ref[:, lanes] * branch
             sums = jnp.where(alive[:, :1], sums, 0.0)
             res[m, :, lanes] = sums.astype(jnp.bfloat16)
 
-        pltpu.make_async_copy(res.at[m], out_ref.at[m], out_sem.at[m]).start()
-
-        @pl.when(jnp.logical_and(m == 0, level < 7))
-        def _():
-            pl.semaphore_wait(ready, 1)
-
-        @pl.when(lax.rem(level, 2) == 0)
-        def _():
-            stat_out[m] = row_stats(res[m])
-
-        @pl.when(level == 0)
-        def _():
-            @pl.when(jnp.logical_or(m > 0, core == 1))
+            @pl.when(prunes)
             def _():
-                pl.semaphore_wait(turn, 1)
-
-            for i in order:
-                token_copy(i, m, res, rows).start()
-            token_copy(1, m, res, rows).wait_send()
-
-            @pl.when(jnp.logical_or(m < micro - 1, core == 0))
-            def _():
-                pl.semaphore_signal(turn, inc=1, device_id=sibling, device_id_type=MESH)
-
-        @pl.when(jnp.logical_and(lax.rem(level, 2) == 1, level < 7))
-        def _():
-            for low in range(0, feats, 4 * LANE):
-                size = min(4 * LANE, feats - low)
-                lanes = slice(low, low + size)
                 taken = lax.dot_general(
                     picks[m], res[m, :, lanes], (((0,), (0,)), ((), ())), preferred_element_type=jnp.float32
                 )
                 pruned[m, :, lanes] = taken.astype(jnp.bfloat16)
+
+            if i == 0:
+                start((0,))
+
+        @pl.when(prunes)
+        def _():
             stat_out[m] = row_stats(pruned[m])
 
-        for here, source, count in outgoing:
-
-            @pl.when(level == here)
+        @pl.when(lax.rem(level, 2) == 0)
+        def _():
+            stat_out[m] = row_stats(res[m])
+
+        start((3, 1, 2))
+        pltpu.make_async_copy(res.at[m], out_ref.at[m], out_sem.at[m]).start()
+
+        @pl.when(level == 0)
+        def _():
+            @pl.when(jnp.logical_or(m > 0, core == 1))
             def _():
-                for i in order:
-                    token_copy(i, m, source, count).start()
+                pl.semaphore_wait(turn, 1)
+
+            for i in order:
+                token_copy(i, m, res, rows).start()
+
+            @pl.when(jnp.logical_and(m == micro - 1, core == 0))
+            def _():
+                token_copy(1, m, res, rows).wait_send()
+                pl.semaphore_signal(turn, inc=1, device_id=sibling, device_id_type=MESH)
 
         return carry
 
@@ -476,6 +514,10 @@
         def _():
             for i in (3, 0, 2):
                 token_copy(i, m, res, rows).wait_send()
+
+            @pl.when(jnp.logical_and(m == micro - 1, core == 1))
+            def _():
+                token_copy(1, m, res, rows).wait_send()
 
         for here, source, count in outgoing:
 
@@ -514,7 +556,8 @@
             pltpu.VMEM((64, feats), jnp.float32),
             pltpu.VMEM((REST, LANE), jnp.float32),
             pltpu.VMEM((rows, feats), jnp.bfloat16),
-            pltpu.VMEM((64 * rows_in, rows), jnp.float32),
+            pltpu.VMEM((AHEAD * rows, feats), jnp.bfloat16),
+            pltpu.VMEM((AHEAD, 64 * rows_in, rows), jnp.float32),
             pltpu.VMEM((64 * rows_out, rows), jnp.float32),
             pltpu.VMEM(every.shape, jnp.bfloat16),
             pltpu.VMEM(rest.shape, jnp.bfloat16),

time: 157 us -> 154 us (0.981)
  Pallas kernels: 152 us -> 149 us
    pallas_call x1, Pallas kernels: 152 us -> 149 us  [shards(): pl.pallas_call(kernel, out_shape=jax.ShapeDtypeStruct((micro, rows, feats...]
where the time goes in v4:
time: 154 us; the launch traced here: 152 us
  Pallas kernels  149 us (97%)
  local copies, waits for them, and re-layouts  2.77 us (2%)
    pallas_call x1, Pallas kernels, shards(): pl.pallas_call(kernel, out_shape=jax.ShapeDtypeStruct((micro, rows, feats...  149 us

profile of v4, /device:TPU:56, one launch (start us, length us, event | category | flops | bytes accessed | tf_op | source)
XLA Modules:
  0.0 152.0 jit_solution(8388041619267428554)
XLA Ops:
  0.0 149.3 %shard_map.100 = bf16[4,128,1664]{2,1,0:T(8,128)(2,1)} custom-call(bf16[4,128,1664]{2,1,0:T(8,128)(2,1)} %bitcast.10, s32[4,96]{1,0:T(4,128)} %bitcast.13, s32[4,64]{1,0:T(4,128)} %bitcast.14, s32[4,48]{1,0:T(4,128)} %bitcast.15, f32[1,1664]{1,0:T(1,128)} %gain_ref.1, f32[1,1664]{1,0:T(1,128)} %scale_ref.1, bf16[39,1664]{1,0:T(8,128)(2,1)} %bitcast.11, ...), custom_call_target="tpu_custom_call" | custom-call | tf_op jit(solution)/shard_map/pallas_call | solution.py:543
  149.3 2.8 %copy.13 = bf16[1,4,1,128,1664]{4,3,2,1,0:T(8,128)(2,1)} copy(bf16[1,4,1,128,1664]{4,3,2,1,0:T(8,128)(2,1)} %bitcast.9) | data formatting | bytes 3407872

commit v5 on v4

--- a/solution.py
+++ b/solution.py
@@ -14,9 +14,9 @@
 LANE = 128
 MAIN = 48
 REST = 64
-A_ROWS = 272
-A_HALF = 144
-B_HALF = 208
+A_ROWS = 240
+A_HALF = 128
+B_HALF = 224
 TOTAL = 13 * MAIN + REST
 LAST = {"x": 2, "z": 4}
 SIGN = (-1, 1)

time: 154 us -> 151 us (0.981)
  Pallas kernels: 149 us -> 146 us
    pallas_call x1, Pallas kernels: 149 us -> 146 us  [shards(): pl.pallas_call(kernel, out_shape=jax.ShapeDtypeStruct((micro, rows, feats...]
where the time goes in v5:
time: 151 us; the launch traced here: 149 us
  Pallas kernels  146 us (97%)
  local copies, waits for them, and re-layouts  2.77 us (2%)
    pallas_call x1, Pallas kernels, shards(): pl.pallas_call(kernel, out_shape=jax.ShapeDtypeStruct((micro, rows, feats...  146 us

profile of v5, /device:TPU:56, one launch (start us, length us, event | category | flops | bytes accessed | tf_op | source)
XLA Modules:
  0.0 149.1 jit_solution(17005181617932905417)
XLA Ops:
  0.0 146.4 %shard_map.100 = bf16[4,128,1664]{2,1,0:T(8,128)(2,1)} custom-call(bf16[4,128,1664]{2,1,0:T(8,128)(2,1)} %bitcast.10, s32[4,96]{1,0:T(4,128)} %bitcast.13, s32[4,64]{1,0:T(4,128)} %bitcast.14, s32[4,48]{1,0:T(4,128)} %bitcast.15, f32[1,1664]{1,0:T(1,128)} %gain_ref.1, f32[1,1664]{1,0:T(1,128)} %scale_ref.1, bf16[39,1664]{1,0:T(8,128)(2,1)} %bitcast.11, ...), custom_call_target="tpu_custom_call" | custom-call | tf_op jit(solution)/shard_map/pallas_call | solution.py:543
  146.4 2.8 %copy.13 = bf16[1,4,1,128,1664]{4,3,2,1,0:T(8,128)(2,1)} copy(bf16[1,4,1,128,1664]{4,3,2,1,0:T(8,128)(2,1)} %bitcast.9) | data formatting | bytes 3407872
